TPU v7x, 32 devices: a whole 2x2x4 slice. The times are simulated.
32 devices in a mesh: peer: 16 (over z, y, x), tp: 2 (over core).
Axes of the slice: x: 2, y: 2, z: 4, core: 2. Of those that a mesh axis runs over, the one named last changes fastest.
Arguments:
- grad_blocks: bfloat16 [6144, 6656], P('peer', 'tp'), may hold values from -6 to 6
- row_scale: float32 [6144], P('peer'), may hold values from 0.25 to 4
- dest_peer: int32 [6144, 1], P('peer'), may hold values from 0 to 15; in each aligned block of 384 rows (0 to 383, 384 to 767, ...) at most 48 rows name the same one
- dest_slot: int32 [6144], P('peer'), may hold values from 0 to 383
- doc_ids: int32 [16, 384], P('peer'), may hold values from 0 to 23, never falling along the last dimension, each value on 1 to 192 neighbouring positions
- query_rows: bfloat16 [6144, 6144], P('peer', 'tp'), may hold values from -21 to 21
- key_rows: bfloat16 [6144, 6144], P('peer', 'tp'), may hold values from -3 to 3
- value_rows: bfloat16 [6144, 6144], P('peer', 'tp'), may hold values from -6 to 6
- out_weight: bfloat16 [6144, 6656], P('tp', 'peer'), may hold values from -0.078125 to 0.078125
Outputs:
- grad_q: bfloat16 [6144, 6144], P('peer', 'tp')
- grad_k: bfloat16 [6144, 6144], P('peer', 'tp')
- grad_v: bfloat16 [6144, 6144], P('peer', 'tp')
Inputs may be any that keep to these rules, and one draw needn't show every extreme that they name: `dest_peer`: no peer is named by more than 48 rows of one device, and in every draw some peer is named by exactly 48 rows of some device. `doc_ids`: along each row of 384 the ids never fall; a document has at most half of 384 positions.
All inputs are finite; a program needn't handle non-finite values.
Results may differ from a plain program's by a relative error of at most 0.014.
Values may be sent and summed in bfloat16 or wider, within the bound.
No kernel may reach another device: no remote copies, remote signals or barrier semaphores. Data moves between devices by JAX's collectives and lax.ppermute only.
A program may use at most 192 MiB of HBM per device.

v0:
```python
import math

import jax
import jax.numpy as jnp
from jax import lax
from jax.sharding import PartitionSpec as P

HS = 128


def attend_local(query_part, key_part, value_part, grad_part, doc_part, head_size):
    count = query_part.shape[0]

    def heads(array):
        return array.reshape(count, -1, head_size)

    q_heads = heads(query_part)
    k_heads = heads(key_part)
    v_heads = heads(value_part)
    g_heads = heads(grad_part)
    factor = 1.0 / math.sqrt(head_size)
    scores = (
        jnp.einsum("ihd,jhd->hij", q_heads, k_heads, preferred_element_type=jnp.float32) * factor
    )
    places = jnp.arange(count, dtype=jnp.int32)
    allowed = (doc_part[:, None] == doc_part[None, :]) & (places[None, :] <= places[:, None])
    scores = jnp.where(allowed[None], scores, -1e30)
    highest = jnp.max(scores, axis=-1, keepdims=True)
    raised = jnp.exp(scores - highest)
    probs = raised / jnp.sum(raised, axis=-1, keepdims=True)
    grad_p = jnp.einsum("ihd,jhd->hij", g_heads, v_heads, preferred_element_type=jnp.float32)
    output = jnp.einsum("hij,jhd->ihd", probs, v_heads.astype(jnp.float32))
    delta = jnp.sum(g_heads.astype(jnp.float32) * output, axis=-1)
    delta_rows = jnp.transpose(delta)[:, :, None]
    probs_low = probs.astype(jnp.bfloat16)
    grad_v = jnp.einsum("hij,ihd->jhd", probs_low, g_heads, preferred_element_type=jnp.float32)
    grad_low = (probs * (grad_p - delta_rows)).astype(jnp.bfloat16)
    grad_q = (
        jnp.einsum("hij,jhd->ihd", grad_low, k_heads, preferred_element_type=jnp.float32) * factor
    )
    grad_k = (
        jnp.einsum("hij,ihd->jhd", grad_low, q_heads, preferred_element_type=jnp.float32) * factor
    )
    return (
        grad_q.reshape(count, -1).astype(jnp.bfloat16),
        grad_k.reshape(count, -1).astype(jnp.bfloat16),
        grad_v.reshape(count, -1).astype(jnp.bfloat16),
    )


def shards(
    grad_blocks,
    row_scale,
    dest_peer,
    dest_slot,
    doc_ids,
    query_rows,
    key_rows,
    value_rows,
    out_weight,
):
    tok_count = grad_blocks.shape[0]
    width_part = grad_blocks.shape[1]
    peer_count = lax.axis_size("peer")
    capacity = 2 * tok_count // peer_count
    target_peer = dest_peer[:, 0]
    one_hot = (target_peer[:, None] == jnp.arange(peer_count, dtype=jnp.int32)[None, :]).astype(
        jnp.int32
    )
    earlier = jnp.cumsum(one_hot, axis=0) - one_hot
    within = jnp.sum(earlier * one_hot, axis=1)
    position = target_peer * capacity + within
    buffer_slots = (
        jnp.full((peer_count * capacity,), -1.0, jnp.float32)
        .at[position]
        .set(dest_slot.astype(jnp.float32))
    )
    scaled = row_scale[:, None] * grad_blocks.astype(jnp.float32)
    buffer_rows = (
        jnp.zeros((peer_count * capacity, width_part), jnp.float32).at[position].set(scaled)
    )
    arrived = (
        lax.all_to_all(
            buffer_rows.reshape(peer_count, capacity, width_part),
            "peer",
            split_axis=0,
            concat_axis=0,
            tiled=True,
        ),
        lax.all_to_all(
            buffer_slots.reshape(peer_count, capacity),
            "peer",
            split_axis=0,
            concat_axis=0,
            tiled=True,
        ),
    )
    arrived_rows = arrived[0].reshape(peer_count * capacity, width_part)
    arrived_slots = arrived[1].reshape(peer_count * capacity).astype(jnp.int32)
    landing = jnp.where(arrived_slots < 0, tok_count, arrived_slots)
    grad_local = (
        jnp.zeros((tok_count, width_part), jnp.float32).at[landing].add(arrived_rows, mode="drop")
    )
    grad_rows = grad_local.astype(jnp.bfloat16)
    full_rows = lax.all_gather(grad_rows, "tp", axis=1, tiled=True)
    grad_attn = lax.dot_general(
        full_rows,
        lax.all_gather(out_weight, "peer", axis=1, tiled=True),
        (((1,), (1,)), ((), ())),
        preferred_element_type=jnp.float32,
    ).astype(jnp.bfloat16)
    return attend_local(query_rows, key_rows, value_rows, grad_attn, doc_ids[0], HS)


def solution(mesh):
    return jax.shard_map(
        shards,
        mesh=mesh,
        in_specs=(
            P("peer", "tp"),
            P("peer"),
            P("peer", None),
            P("peer"),
            P("peer", None),
            P("peer", "tp"),
            P("peer", "tp"),
            P("peer", "tp"),
            P("tp", "peer"),
        ),
        out_specs=(P("peer", "tp"), P("peer", "tp"), P("peer", "tp")),
        check_vma=False,
    )
```

profile of v0, /device:TPU:0, one launch (start us, length us, event | category | flops | bytes accessed | tf_op | source)
XLA Modules:
  0.0 826.8 jit_solution(5753645103723724841)
XLA Ops:
  10.5 2.9 scatter_custom_fusion
  14.1 8.3 %all-to-all-start = ((f32[16,1,48]{2,1,0:T(1,128)}), f32[16,1,48]{2,1,0:T(1,128)S(1)}, u32[]{:S(2)}, u32[]{:S(2)}) async-start(f32[16,1,48]{2,1,0:T(1,128)} %all_to_all.9), calls=%async_computation | async-start | bytes 16384 | tf_op jit(solution)/shard_map/all_to_all | solution.py:90
  22.4 9.4 %scatter_custom_fusion.1 = f32[768,3328]{1,0:T(8,128)} fusion(s32[384]{0:T(512)S(1)} %fusion.24, bf16[384,3328]{1,0:T(8,128)(2,1)} %param.9, f32[]{:T(128)} %constant.12.clone.1, f32[384]{0:T(512)} %param.10), kind=kCustom, calls=%fused_computation.11 | custom fusion | flops 2555904 | bytes 12781060 | tf_op jit(solution)/shard_map/scatter | solution.py:80
  31.9 7.0 all-to-all-start.1
  39.2 190.9 %all-to-all-done.1 = f32[16,48,3328]{2,1,0:T(8,128)} async-done(((f32[16,48,3328]{2,1,0:T(8,128)}), f32[16,48,3328]{2,1,0:T(8,128)}, u32[]{:S(2)}, u32[]{:S(2)}) %all-to-all-start.1) | async-done | bytes 10223648 | tf_op jit(solution)/shard_map/all_to_all | solution.py:83
  230.1 24.5 %scatter_custom_fusion.2 = f32[384,3328]{1,0:T(8,128)} fusion(s32[768]{0:T(1024)S(1)} %fusion.21, f32[768,3328]{1,0:T(8,128)} %bitcast.2, f32[]{:T(128)} %constant.12.clone.1), kind=kCustom, calls=%fused_computation.21 | custom fusion | flops 2555904 | bytes 5112320 | tf_op jit(solution)/shard_map/scatter-add | solution.py:102
  254.6 4.1 convert_element_type.75
  259.6 3.0 copy.52
  262.6 4.7 copy.55
  267.3 4.3 copy.53
  271.7 9.2 %fusion = (f32[24,384]{1,0:T(8,128)S(1)}, f32[24,384,384]{1,2,0:T(8,128)}) fusion(pred[384,384]{0,1:T(8,128)(4,1)S(1)} %fusion.16, bf16[384,24,128]{0,2,1:T(8,128)(2,1)} %bitcast.59, bf16[384,24,128]{0,2,1:T(8,128)(2,1)S(1)} %bitcast.56), kind=kOutput, calls=%fused_computation.6 | convolution fusion | flops 916577280 | bytes 19058688 | tf_op jit(solution)/shard_map/ihd,jhd->hij/dot_general | solution.py:23
  280.9 7.9 fusion.2
  288.9 25.0 %all-gather.3.cloned.1.call-done = bf16[384,6656]{1,0:T(8,128)(2,1)} async-done(((bf16[384,3328]{1,0:T(8,128)(2,1)}), bf16[384,6656]{1,0:T(8,128)(2,1)}) %all-gather.3.cloned.1.call-update) | async-done | bytes 5111824 | tf_op jit(solution)/shard_map/all_gather | solution.py:105
  313.9 424.2 %all-gather.5.cloned.1.call-done = bf16[3072,6656]{0,1:T(8,128)(2,1)} async-done(((bf16[3072,416]{0,1:T(8,128)(2,1)}), bf16[3072,6656]{0,1:T(8,128)(2,1)}) %all-gather.5.cloned.1.call-update) | async-done | bytes 40894480 | tf_op jit(solution)/shard_map/all_gather | solution.py:108
  738.1 23.6 %convolution_convert_fusion = bf16[384,3072]{1,0:T(8,128)(2,1)} fusion(bf16[384,6656]{1,0:T(8,128)(2,1)} %all-gather.3.cloned.1.call-done, bf16[3072,6656]{0,1:T(8,128)(2,1)} %all-gather.5.cloned.1.call-done), kind=kOutput, calls=%fused_computation.19 | convolution fusion | flops 15704653824 | bytes 48365568 | tf_op jit(solution)/shard_map/dot_general | solution.py:106
  761.6 4.3 copy.54
  765.9 8.3 %fusion.9 = f32[384,24]{0,1:T(8,128)S(1)} fusion(bf16[384,24,128]{0,2,1:T(8,128)(2,1)} %bitcast.63, bf16[384,24,128]{0,2,1:T(8,128)(2,1)S(1)} %bitcast.61, f32[24,384,384]{1,2,0:T(8,128)} %get-tuple-element.10, f32[24,384]{1,0:T(8,128)S(1)} %fusion.2, f32[24,384]{1,0:T(8,128)S(1)} %get-tuple-element.9, pred[384,384]{0,1:T(8,128)(4,1)S(1)} %fusion.16), kind=kOutput, calls=%fused_computation.16 | convolution fusion | flops 923655168 | bytes 19132416 | tf_op jit(solution)/shard_map/hij,jhd->ihd/dot_general | solution.py:32
  774.2 11.9 %multiply_convert_fusion = bf16[24,384,384]{1,2,0:T(8,128)(2,1)} fusion(bf16[384,24,128]{0,2,1:T(8,128)(2,1)} %bitcast.64, bf16[384,24,128]{0,2,1:T(8,128)(2,1)S(1)} %bitcast.62, f32[24,384]{1,0:T(8,128)S(1)} %bitcast.70, f32[24,384]{1,0:T(8,128)S(1)} %fusion.2, f32[24,384]{1,0:T(8,128)S(1)} %get-tuple-element.9, f32[24,384,384]{1,2,0:T(8,128)} %get-tuple-element.10, ...), kind=kOutput, calls=%fused_computation.3 | convolution fusion | flops 930742272 | bytes 26210304 | tf_op jit(solution)/shard_map/ihd,jhd->hij/dot_general | solution.py:31
  786.2 7.0 multiply_convert_fusion.2
  793.2 7.6 multiply_convert_fusion.1
  800.9 7.4 fusion.13
  808.2 4.4 copy.44
  812.7 2.6 copy.45
  815.3 4.3 copy.46
  (38 shorter events, 5.3 us)
Async XLA Ops:
  14.1 17.8 %all-to-all-start = ((f32[16,1,48]{2,1,0:T(1,128)}), f32[16,1,48]{2,1,0:T(1,128)S(1)}, u32[]{:S(2)}, u32[]{:S(2)}) async-start(f32[16,1,48]{2,1,0:T(1,128)} %all_to_all.9), calls=%async_computation | async-start | bytes 16384 | tf_op jit(solution)/shard_map/all_to_all | solution.py:90
  31.9 198.2 %all-to-all-start.1 = ((f32[16,48,3328]{2,1,0:T(8,128)}), f32[16,48,3328]{2,1,0:T(8,128)}, u32[]{:S(2)}, u32[]{:S(2)}) async-start(f32[16,48,3328]{2,1,0:T(8,128)} %bitcast.55), calls=%async_computation.1 | async-start | bytes 20447232 | tf_op jit(solution)/shard_map/all_to_all | solution.py:83
  38.8 275.1 %all-gather.3.cloned.1.call-start = ((), (), s32[]{:S(2)}) async-start(), calls=%async_computation.2 | async-start | bytes 7667712 | tf_op jit(solution)/shard_map/all_gather | solution.py:105
  258.8 479.3 %all-gather.5.cloned.1.call-start = ((), (), s32[]{:S(2)}) async-start(), calls=%async_computation.3 | async-start | bytes 43450368 | tf_op jit(solution)/shard_map/all_gather | solution.py:108
  259.6 7.7 copy-start.4
  262.6 18.4 %copy-start = (bf16[384,3072]{0,1:T(8,128)(2,1)}, bf16[384,3072]{0,1:T(8,128)(2,1)S(1)}, u32[]{:S(2)}) copy-start(bf16[384,3072]{0,1:T(8,128)(2,1)S(1)} %copy.52) | copy-start | bytes 7077892
  288.9 477.0 %copy-start.2 = (bf16[384,3072]{0,1:T(8,128)(2,1)S(1)}, bf16[384,3072]{0,1:T(8,128)(2,1)}, u32[]{:S(2)}) copy-start(bf16[384,3072]{0,1:T(8,128)(2,1)} %copy.55) | copy-start | bytes 7077892
  786.2 7.0 copy-start.1
  786.2 14.6 %slice-start = ((s8[14155776]{0:T(1024)(128)(4,1)}), s8[4194304]{0:T(1024)(128)(4,1)S(1)}, s32[]{:S(2)}) async-start(s8[14155776]{0:T(1024)(128)(4,1)} %bitcast.53), calls=%async_computation.4 | async-start | bytes 8388608
  786.2 14.6 %slice-start.1 = ((s8[14155776]{0:T(1024)(128)(4,1)}), s8[4194304]{0:T(1024)(128)(4,1)S(1)}, s32[]{:S(2)}) async-start(s8[14155776]{0:T(1024)(128)(4,1)} %bitcast.53), calls=%async_computation.5 | async-start | bytes 8388608
  786.2 14.6 %slice-start.2 = ((s8[14155776]{0:T(1024)(128)(4,1)}), s8[4194304]{0:T(1024)(128)(4,1)S(1)}, s32[]{:S(2)}) async-start(s8[14155776]{0:T(1024)(128)(4,1)} %bitcast.53), calls=%async_computation.6 | async-start | bytes 8388608
  793.2 7.6 slice-start.3
  808.2 4.4 copy-start.3
Sparse Core Ops, SparseCore 0:
  258.9 54.9 all-gather.2
  316.7 421.3 all-gather.4
where the time goes:
time: 833 us; the launch traced here: 827 us
  waiting for transfers between devices  641 us (77%)
  matrix products  75.1 us (9%)
  other arithmetic  49.3 us (6%)
  local copies, waits for them, and re-layouts  31.4 us (4%)
  starting transfers between devices  15.7 us (2%)
  between operations  14.6 us (2%)
    all_gather x1, waiting for transfers between devices, shards(): lax.all_gather(out_weight, 'peer', axis=1, tiled=True)  424 us
    all_to_all x1, waiting for transfers between devices, shards(): lax.all_to_all(buffer_rows.reshape(peer_count, capacity, width_part), 'pe...  191 us
    all_gather x1, waiting for transfers between devices, shards(): full_rows = lax.all_gather(grad_rows, 'tp', axis=1, tiled=True)  25 us
    scatter-add x1, other arithmetic, shards(): jnp.zeros((tok_count, width_part), jnp.float32).at[landing]  24.5 us
    dot_general x1, matrix products, shards(): lax.dot_general(full_rows, lax.all_gather(out_weight, 'peer', axis=1, til...  23.6 us
  transfers between devices with their start and end apart: 4, of which 3 were waited for; matrix products, arithmetic and copies ran while one was open for 5% of the time, Pallas kernels for 0%

commit v1 on v0

v1 whole, which is shorter than its diff:
```python
import functools
import math

import jax
import jax.numpy as jnp
from jax import lax
from jax.experimental import pallas as pl
from jax.experimental.pallas import tpu as pltpu
from jax.sharding import PartitionSpec as P

HS = 128
INNER = 4
AXES = ("peer", "tp")
PARAMS = pltpu.CompilerParams(vmem_limit_bytes=56 * 1024 * 1024)


def swap(array, peers, cores, move):
    pairs = []
    for peer in range(peers):
        for core in range(cores):
            to_peer, to_core = move(peer, core)
            pairs.append((peer * cores + core, to_peer * cores + to_core))
    return lax.ppermute(array, AXES, pairs)


def after(array, *others):
    return lax.optimization_barrier((array,) + others)[0]


def pack_kernel(position_ref, rows_ref, *out_refs):
    count = out_refs[0].shape[0]
    rows = rows_ref[...]
    for k, out_ref in enumerate(out_refs):
        places = lax.broadcasted_iota(jnp.int32, (count, rows.shape[0]), 0) + k * count
        chosen = (places == position_ref[...]).astype(jnp.float32).astype(jnp.bfloat16)
        out_ref[...] = jnp.dot(chosen, rows, preferred_element_type=jnp.float32).astype(jnp.bfloat16)


def pack(position, rows, parts, count):
    width = rows.shape[1]
    return pl.pallas_call(
        pack_kernel,
        out_shape=[jax.ShapeDtypeStruct((count, width), jnp.bfloat16)] * parts,
        compiler_params=PARAMS,
        cost_estimate=pl.CostEstimate(
            flops=2 * parts * count * rows.size, bytes_accessed=2 * (rows.size + parts * count * width), transcendentals=0
        ),
    )(position[None, :], rows)


def place_kernel(slots_ref, *refs):
    out_ref = refs[-1]
    rows = jnp.concatenate([ref[0] for ref in refs[:-1]], axis=0)
    tokens = lax.broadcasted_iota(jnp.int32, (out_ref.shape[1], rows.shape[0]), 0)
    chosen = (tokens == slots_ref[0]).astype(jnp.float32).astype(jnp.bfloat16)
    out_ref[0] = jnp.dot(chosen, rows, preferred_element_type=jnp.float32).astype(jnp.bfloat16)


def place(slots, pieces, tok_count):
    groups, capacity, width = pieces[0].shape
    total = slots.shape[2]
    return pl.pallas_call(
        place_kernel,
        grid=(groups,),
        in_specs=[pl.BlockSpec((1, 1, total), lambda t: (t, 0, 0))]
        + [pl.BlockSpec((1, capacity, width), lambda t: (t, 0, 0))] * len(pieces),
        out_specs=pl.BlockSpec((1, tok_count, width), lambda t: (t, 0, 0)),
        out_shape=jax.ShapeDtypeStruct((groups, tok_count, width), jnp.bfloat16),
        compiler_params=PARAMS,
        cost_estimate=pl.CostEstimate(
            flops=2 * groups * tok_count * total * width,
            bytes_accessed=2 * groups * width * (total + tok_count),
            transcendentals=0,
        ),
    )(slots, *pieces)


def join_kernel(own_ref, *refs):
    out_ref = refs[-1]
    for k, ref in enumerate(refs[:-1]):
        out_ref[k ^ own_ref[0]] = ref[...]


def join(own, pieces):
    depth, columns = pieces[0].shape
    joined = pl.pallas_call(
        join_kernel,
        in_specs=[pl.BlockSpec(memory_space=pltpu.SMEM)]
        + [pl.BlockSpec((depth, columns), lambda: (0, 0))] * len(pieces),
        out_shape=jax.ShapeDtypeStruct((len(pieces), depth, columns), jnp.bfloat16),
        compiler_params=PARAMS,
        cost_estimate=pl.CostEstimate(
            flops=0, bytes_accessed=4 * len(pieces) * depth * columns, transcendentals=0
        ),
    )(own.reshape(1), *pieces)
    return joined.reshape(len(pieces) * depth, columns)


def product_kernel(rows_ref, weight_ref, *refs):
    total = jnp.dot(rows_ref[0], weight_ref[...], preferred_element_type=jnp.float32)
    for ref in refs[:-1]:
        total = total + ref[0].astype(jnp.float32)
    refs[-1][0] = total.astype(jnp.bfloat16)


def product(rows, weight, block, columns, level, arrived):
    groups, tok_count, width = rows.shape
    first, step = 1 << level, 2 << level
    steps = groups // step
    in_specs = [
        pl.BlockSpec((1, tok_count, width), lambda m: (first + m * step, 0, 0)),
        pl.BlockSpec((width, columns), lambda m: (0, block)),
    ]
    for j in range(level):
        in_specs.append(
            pl.BlockSpec((1, tok_count, columns), lambda m, j=j: ((first >> (j + 1)) + m * (step >> (j + 1)), 0, 0))
        )
    return pl.pallas_call(
        product_kernel,
        grid=(steps,),
        in_specs=in_specs,
        out_specs=pl.BlockSpec((1, tok_count, columns), lambda m: (m, 0, 0)),
        out_shape=jax.ShapeDtypeStruct((steps, tok_count, columns), jnp.bfloat16),
        compiler_params=PARAMS,
        cost_estimate=pl.CostEstimate(
            flops=2 * steps * tok_count * width * columns,
            bytes_accessed=2 * (steps * tok_count * (width + columns) + width * columns),
            transcendentals=0,
        ),
    )(rows, weight, *arrived)


def attend_kernel(n_arrived, n_old, rows_ref, weight_ref, doc_ref, doc_column_ref, q_ref, k_ref, v_ref, *refs):
    arrived = refs[:n_arrived]
    dq_ref, dk_ref, dv_ref = refs[n_arrived + n_old :]
    total = jnp.dot(rows_ref[0], weight_ref[...], preferred_element_type=jnp.float32)
    for ref in arrived:
        total = total + ref[0].astype(jnp.float32)
    grad = total.astype(jnp.bfloat16)
    q, k, v = q_ref[...], k_ref[...], v_ref[...]
    count = q.shape[0]
    factor = 1.0 / math.sqrt(HS)
    across = (((1,), (1,)), ((), ()))
    down = (((0,), (0,)), ((), ()))
    scores = lax.dot_general(k, q, across, preferred_element_type=jnp.float32) * factor
    key_at = lax.broadcasted_iota(jnp.int32, (count, count), 0)
    query_at = lax.broadcasted_iota(jnp.int32, (count, count), 1)
    allowed = (doc_column_ref[...] == doc_ref[...]) & (key_at <= query_at)
    scores = jnp.where(allowed, scores, -1e30)
    raised = jnp.exp(scores - jnp.max(scores, axis=0, keepdims=True))
    probs = raised * (1.0 / jnp.sum(raised, axis=0, keepdims=True))
    grad_p = lax.dot_general(v, grad, across, preferred_element_type=jnp.float32)
    delta = jnp.sum(probs * grad_p, axis=0, keepdims=True)
    grad_s = (probs * (grad_p - delta)).astype(jnp.bfloat16)
    probs_low = probs.astype(jnp.bfloat16)
    dv_ref[...] = jnp.dot(probs_low, grad, preferred_element_type=jnp.float32).astype(jnp.bfloat16)
    dk = jnp.dot(grad_s, q, preferred_element_type=jnp.float32) * factor
    dk_ref[...] = dk.astype(jnp.bfloat16)
    dq = lax.dot_general(grad_s, k, down, preferred_element_type=jnp.float32) * factor
    dq_ref[...] = dq.astype(jnp.bfloat16)


def attend(rows, weight, first_block, first_head, heads, arrived, doc, query, key, value, old):
    tok_count, features = query.shape
    width = rows.shape[2]
    head_spec = pl.BlockSpec((tok_count, HS), lambda h: (0, first_head + h))
    in_specs = [
        pl.BlockSpec((1, tok_count, width), lambda h: (0, 0, 0)),
        pl.BlockSpec((width, HS), lambda h: (0, first_block + h)),
        pl.BlockSpec((1, tok_count), lambda h: (0, 0)),
        pl.BlockSpec((tok_count, 1), lambda h: (0, 0)),
        head_spec,
        head_spec,
        head_spec,
    ]
    in_specs += [pl.BlockSpec((1, tok_count, HS), lambda h: (0, 0, h))] * len(arrived)
    in_specs += [pl.BlockSpec(memory_space=pl.ANY)] * len(old)
    base = 7 + len(arrived)
    return pl.pallas_call(
        functools.partial(attend_kernel, len(arrived), len(old)),
        grid=(heads,),
        in_specs=in_specs,
        out_specs=[head_spec] * 3,
        out_shape=[jax.ShapeDtypeStruct((tok_count, features), jnp.bfloat16)] * 3,
        input_output_aliases={base + n: n for n in range(len(old))},
        compiler_params=PARAMS,
        cost_estimate=pl.CostEstimate(
            flops=2 * heads * tok_count * HS * (width + 5 * tok_count),
            bytes_accessed=2 * heads * HS * (width + 8 * tok_count) + 2 * tok_count * width,
            transcendentals=heads * tok_count * tok_count,
        ),
    )(rows, weight, doc, doc.reshape(tok_count, 1), query, key, value, *arrived, *old)


def shards(
    grad_blocks,
    row_scale,
    dest_peer,
    dest_slot,
    doc_ids,
    query_rows,
    key_rows,
    value_rows,
    out_weight,
):
    tok_count, width_part = grad_blocks.shape
    peers, cores = lax.axis_size("peer"), lax.axis_size("tp")
    planes = peers // INNER
    span = planes // cores
    width = width_part // span
    capacity = 2 * tok_count // peers
    room = -(-capacity // 16) * 16
    levels = planes.bit_length() - 1
    me, core = lax.axis_index("peer"), lax.axis_index("tp")
    plane, inner = me // INNER, me % INNER
    send = functools.partial(swap, peers=peers, cores=cores)

    known = (dest_peer[:, 0] * tok_count + dest_slot)[None, :]
    step = 1
    while step < peers:
        known = jnp.concatenate([known, send(known, move=lambda p, c: (p ^ step, c))], axis=0)
        step *= 2

    plane_rows = []
    for r in range(span):
        start = ((plane % span) ^ r) * width
        part = lax.dynamic_slice(grad_blocks, (0, start), (tok_count, width))
        part = (row_scale[:, None] * part.astype(jnp.float32)).astype(jnp.bfloat16)

        def move(p, c, r=r):
            o, i = p // INNER, p % INNER
            return (c * span + ((o % span) ^ r)) * INNER + i, o // span

        plane_rows.append(send(part, move=move))

    weight = out_weight.T
    n_heads = weight.shape[1] // HS
    chunk = n_heads // 6
    n_groups, per_group = 3, 2
    group_columns = chunk * per_group * HS

    def gather_weight(g, *hold):
        part = weight[:, g * group_columns : (g + 1) * group_columns]
        if hold:
            part = after(part, *hold)
        pieces = [part] + [send(part, move=lambda p, c, k=k: (p ^ k, c)) for k in range(1, INNER)]
        return join(inner, pieces)

    weights = [gather_weight(0)]

    offset = core ^ (plane // span)
    known = known.reshape(cores, span, INNER, tok_count)[offset ^ jnp.arange(cores, dtype=jnp.int32)]
    known = known.reshape(peers, tok_count)
    target, slot = known // tok_count, known % tok_count
    rows_at = jnp.arange(tok_count, dtype=jnp.int32)
    same = (target[:, :, None] == target[:, None, :]) & (rows_at[None, None, :] < rows_at[None, :, None])
    within = jnp.sum(same.astype(jnp.int32), axis=2)
    groups = ((plane ^ jnp.arange(planes, dtype=jnp.int32)) * INNER + inner)[:, None, None, None]
    here = (target[None, :, None, :] == groups) & (
        within[None, :, None, :] == jnp.arange(room, dtype=jnp.int32)[None, None, :, None]
    )
    slots = jnp.max(jnp.where(here, slot[None, :, None, :], -1), axis=3).reshape(planes, 1, peers * room)
    position = (((target % INNER) ^ inner) * planes + ((target // INNER) ^ plane)) * room + within

    pieces = [[[None] * INNER for _ in range(span)] for _ in range(cores)]
    for r in range(span):
        packed = pack(position[r * INNER], plane_rows[r], INNER, planes * room)
        for k in range(INNER):
            piece = packed[k] if k == 0 else send(packed[k], move=lambda p, c: (p ^ k, c))
            held = [piece]
            step = 1
            while step < cores:
                held = held + [send(one, move=lambda p, c: (p, c ^ step)) for one in held]
                step *= 2
            for n, one in enumerate(held):
                pieces[n][r][k] = one.reshape(planes, room, width)
    rows = place(slots, [one for by_core in pieces for by_plane in by_core for one in by_plane], tok_count)

    for g in range(1, n_groups):
        weights.append(gather_weight(g, pieces[0][span - 1][INNER - 1]))

    old, first = [], []
    for n in range(n_groups * per_group):
        group, block = n // per_group, n % per_group
        arrived = []
        for level in range(levels):
            part = product(rows, weights[group], block, chunk * HS, level, arrived)
            if level == 0 and n >= 2:
                part = after(part, first[n - 2])
            arrived.append(send(part, move=lambda p, c: (p ^ (INNER << level), c)))
        first.append(arrived[0])
        old = attend(
            rows, weights[group], block * chunk, n * chunk, chunk, arrived,
            doc_ids, query_rows, key_rows, value_rows, old,
        )
    return tuple(old)


def solution(mesh):
    return jax.shard_map(
        shards,
        mesh=mesh,
        in_specs=(
            P("peer", "tp"),
            P("peer"),
            P("peer", None),
            P("peer"),
            P("peer", None),
            P("peer", "tp"),
            P("peer", "tp"),
            P("peer", "tp"),
            P("tp", "peer"),
        ),
        out_specs=(P("peer", "tp"), P("peer", "tp"), P("peer", "tp")),
        check_vma=False,
    )
```

time: 833 us -> 365 us (0.44)
  waiting for transfers between devices: 641 us -> 140 us
  Pallas kernels: 0 us -> 125 us
  matrix products: 75.1 us -> 0 us
  starting transfers between devices: 15.7 us -> 60.7 us
  other arithmetic: 49.3 us -> 15.1 us
  between operations: 14.6 us -> 1.14 us
  local copies, waits for them, and re-layouts: 31.4 us -> 21.5 us
    all_gather x2 -> x0, waiting for transfers between devices: 449 us -> none  [the longest x1 424 us: shards(): lax.all_gather(out_weight, 'peer', axis=1, tiled=True)]
    all_to_all x2 -> x0, waiting for transfers between devices: 191 us -> none  [the longest x1 191 us: shards(): lax.all_to_all(buffer_rows.reshape(peer_count, capacity, width_part), 'pe...]
    ppermute x0 -> x41, waiting for transfers between devices: none -> 140 us  [swap(): return lax.ppermute(array, AXES, pairs)]
    pallas_call x0 -> x24, Pallas kernels: none -> 125 us  [the longest x6 49.3 us: attend(): pl.pallas_call(functools.partial(attend_kernel, len(arrived), len(old)),...]
    dot_general x7 -> x0, matrix products: 75.1 us -> none  [the longest x1 23.6 us: shards(): lax.dot_general(full_rows, lax.all_gather(out_weight, 'peer', axis=1, til...]
    ppermute x0 -> x41, starting transfers between devices: none -> 60.7 us  [swap(): return lax.ppermute(array, AXES, pairs)]
    scatter-add x1 -> x0, other arithmetic: 24.5 us -> none  [shards(): jnp.zeros((tok_count, width_part), jnp.float32).at[landing]]
    all_to_all x2 -> x0, starting transfers between devices: 15.3 us -> none  [the longest x1 8.31 us: shards(): lax.all_to_all(buffer_slots.reshape(peer_count, capacity), 'peer', split_...]
  transfers between devices with their start and end apart: 4 -> 41, of which waited for: 3 -> 15; matrix products, arithmetic and copies ran while one was open for 5% -> 7% of each run, Pallas kernels for 0% -> 32%
where the time goes in v1:
time: 365 us; the launch traced here: 363 us
  waiting for transfers between devices  140 us (38%)
  Pallas kernels  125 us (34%)
  starting transfers between devices  60.7 us (17%)
  local copies, waits for them, and re-layouts  21.5 us (6%)
  other arithmetic  15.1 us (4%)
    ppermute x41, waiting for transfers between devices, swap(): return lax.ppermute(array, AXES, pairs)  140 us
    ppermute x41, starting transfers between devices, swap(): return lax.ppermute(array, AXES, pairs)  60.7 us
    pallas_call x6, Pallas kernels, attend(): pl.pallas_call(functools.partial(attend_kernel, len(arrived), len(old)),...  49.3 us
    pallas_call x12, Pallas kernels, product(): pl.pallas_call(product_kernel, grid=(steps,), in_specs=in_specs, out_spec...  47.4 us
    pallas_call x3, Pallas kernels, join(): pl.pallas_call(join_kernel, in_specs=[pl.BlockSpec(memory_space=pltpu.SME...  11.7 us
    pallas_call x1, Pallas kernels, place(): pl.pallas_call(place_kernel, grid=(groups,), in_specs=[pl.BlockSpec((1, 1...  8.98 us
    unnamed x68, local copies, waits for them, and re-layouts  7.47 us
    pallas_call x2, Pallas kernels, pack(): pl.pallas_call(pack_kernel, out_shape=[jax.ShapeDtypeStruct((count, width...  7.44 us
  transfers between devices with their start and end apart: 41, of which 15 were waited for; matrix products, arithmetic and copies ran while one was open for 7% of the time, Pallas kernels for 32%

profile of v1, /device:TPU:0, one launch (start us, length us, event | category | flops | bytes accessed | tf_op | source)
XLA Modules:
  0.0 363.3 jit_solution(7772243665108471852)
XLA Ops:
  14.6 28.4 %collective-permute-done = s32[1,384]{1,0:T(1,128)S(1)} collective-permute-done((s32[1,384]{1,0:T(1,128)S(1)}, s32[1,384]{1,0:T(1,128)S(1)}, u32[]{:S(2)}, u32[]{:S(2)}) %collective-permute-start) | collective-permute-done | bytes 1568 | tf_op jit(solution)/shard_map/ppermute | solution.py:23
  58.6 11.2 %collective-permute-start.4 = (bf16[384,1664]{1,0:T(8,128)(2,1)}, bf16[384,1664]{1,0:T(8,128)(2,1)}, u32[]{:S(2)}, u32[]{:S(2)}) collective-permute-start(bf16[384,1664]{1,0:T(8,128)(2,1)} %get-tuple-element.62), channel_id=1, source_target_pairs={{0,0},{1,16},{2,2},{3,18},{4,4},{5,20},{6,6},{7,22},{8,8},{9,24},{... | collective-permute-start | bytes 3833864 | tf_op jit(solution)/shard_map/ppermute | solution.py:23
  99.8 8.6 %collective-permute-done.9 = bf16[192,1664]{1,0:T(8,128)(2,1)S(1)} collective-permute-done((bf16[192,1664]{1,0:T(8,128)(2,1)}, bf16[192,1664]{1,0:T(8,128)(2,1)S(1)}, u32[]{:S(2)}, u32[]{:S(2)}) %collective-permute-start.9) | collective-permute-done | bytes 639008 | tf_op jit(solution)/shard_map/ppermute | solution.py:23
  110.1 6.0 %collective-permute-done.10 = bf16[192,1664]{1,0:T(8,128)(2,1)} collective-permute-done((bf16[192,1664]{1,0:T(8,128)(2,1)}, bf16[192,1664]{1,0:T(8,128)(2,1)}, u32[]{:S(2)}, u32[]{:S(2)}) %collective-permute-start.10) | collective-permute-done | bytes 639008 | tf_op jit(solution)/shard_map/ppermute | solution.py:23
  117.3 6.1 %collective-permute-done.11 = bf16[192,1664]{1,0:T(8,128)(2,1)} collective-permute-done((bf16[192,1664]{1,0:T(8,128)(2,1)}, bf16[192,1664]{1,0:T(8,128)(2,1)}, u32[]{:S(2)}, u32[]{:S(2)}) %collective-permute-start.11) | collective-permute-done | bytes 639008 | tf_op jit(solution)/shard_map/ppermute | solution.py:23
  124.0 11.3 %collective-permute-done.5 = bf16[192,1664]{1,0:T(8,128)(2,1)S(1)} collective-permute-done((bf16[192,1664]{1,0:T(8,128)(2,1)}, bf16[192,1664]{1,0:T(8,128)(2,1)S(1)}, u32[]{:S(2)}, u32[]{:S(2)}) %collective-permute-start.5) | collective-permute-done | bytes 639008 | tf_op jit(solution)/shard_map/ppermute | solution.py:23
  135.3 8.1 %collective-permute-done.6 = bf16[192,1664]{1,0:T(8,128)(2,1)} collective-permute-done((bf16[192,1664]{1,0:T(8,128)(2,1)}, bf16[192,1664]{1,0:T(8,128)(2,1)}, u32[]{:S(2)}, u32[]{:S(2)}) %collective-permute-start.6) | collective-permute-done | bytes 639008 | tf_op jit(solution)/shard_map/ppermute | solution.py:23
  154.3 9.0 %shard_map.114.rows_ref = bf16[4,384,1664]{2,1,0:T(8,128)(2,1)} custom-call(s32[4,1,768]{2,1,0:T(1,128)} %reshape.206.slots_ref, bf16[4,48,1664]{2,1,0:T(8,128)(2,1)} %bitcast.46, bf16[4,48,1664]{2,1,0:T(8,128)(2,1)} %bitcast.47, bf16[4,48,1664]{2,1,0:T(8,128)(2,1)} %bitcast.3.refs_2_, bf16[4,48,1664]{2,1,0:T(8,128)(2,1)} %bitcast.4.refs_3_, ...), custom_call_target="tpu_custom_call" | custom-call | flops 3925868544 | bytes 15335424 | tf_op jit(solution)/shard_map/pallas_call | solution.py:62
  163.3 4.4 %shard_map.124 = bf16[2,384,512]{2,1,0:T(8,128)(2,1)} custom-call(bf16[4,384,1664]{2,1,0:T(8,128)(2,1)} %shard_map.114.rows_ref, bf16[1664,1024]{1,0:T(8,128)(2,1)} %bitcast.24), custom_call_target="tpu_custom_call" | custom-call | flops 1308622848 | bytes 5046272 | tf_op jit(solution)/shard_map/pallas_call | solution.py:118
  169.3 4.4 %shard_map.120 = bf16[2,384,512]{2,1,0:T(8,128)(2,1)} custom-call(bf16[4,384,1664]{2,1,0:T(8,128)(2,1)} %shard_map.114.rows_ref, bf16[1664,1024]{1,0:T(8,128)(2,1)} %bitcast.25), custom_call_target="tpu_custom_call" | custom-call | flops 1308622848 | bytes 5046272 | tf_op jit(solution)/shard_map/pallas_call | solution.py:118
  175.1 13.9 %collective-permute-done.24.refs_2_ = bf16[416,1024]{1,0:T(8,128)(2,1)S(1)} collective-permute-done((bf16[416,1024]{1,0:T(8,128)(2,1)S(1)}, bf16[416,1024]{1,0:T(8,128)(2,1)S(1)}, u32[]{:S(2)}, u32[]{:S(2)}) %collective-permute-start.24) | collective-permute-done | bytes 852000 | tf_op jit(solution)/shard_map/ppermute | solution.py:23
  197.4 4.4 %shard_map.123 = bf16[2,384,512]{2,1,0:T(8,128)(2,1)} custom-call(bf16[4,384,1664]{2,1,0:T(8,128)(2,1)} %shard_map.114.rows_ref, bf16[1664,1024]{1,0:T(8,128)(2,1)} %bitcast.30), custom_call_target="tpu_custom_call" | custom-call | flops 1308622848 | bytes 5046272 | tf_op jit(solution)/shard_map/pallas_call | solution.py:118
  203.4 4.4 %shard_map.118 = bf16[2,384,512]{2,1,0:T(8,128)(2,1)} custom-call(bf16[4,384,1664]{2,1,0:T(8,128)(2,1)} %shard_map.114.rows_ref, bf16[1664,1024]{1,0:T(8,128)(2,1)} %bitcast.31), custom_call_target="tpu_custom_call" | custom-call | flops 1308622848 | bytes 5046272 | tf_op jit(solution)/shard_map/pallas_call | solution.py:118
  210.0 17.7 %collective-permute-done.22.refs_3_ = bf16[416,1024]{1,0:T(8,128)(2,1)S(1)} collective-permute-done((bf16[416,1024]{1,0:T(8,128)(2,1)S(1)}, bf16[416,1024]{1,0:T(8,128)(2,1)S(1)}, u32[]{:S(2)}, u32[]{:S(2)}) %collective-permute-start.22) | collective-permute-done | bytes 852000 | tf_op jit(solution)/shard_map/ppermute | solution.py:23
  232.5 4.4 %shard_map.122 = bf16[2,384,512]{2,1,0:T(8,128)(2,1)} custom-call(bf16[4,384,1664]{2,1,0:T(8,128)(2,1)} %shard_map.114.rows_ref, bf16[1664,1024]{1,0:T(8,128)(2,1)} %bitcast.36), custom_call_target="tpu_custom_call" | custom-call | flops 1308622848 | bytes 5046272 | tf_op jit(solution)/shard_map/pallas_call | solution.py:118
  238.4 4.4 %shard_map.116 = bf16[2,384,512]{2,1,0:T(8,128)(2,1)} custom-call(bf16[4,384,1664]{2,1,0:T(8,128)(2,1)} %shard_map.114.rows_ref, bf16[1664,1024]{1,0:T(8,128)(2,1)} %bitcast.37), custom_call_target="tpu_custom_call" | custom-call | flops 1308622848 | bytes 5046272 | tf_op jit(solution)/shard_map/pallas_call | solution.py:118
  261.9 20.2 %collective-permute-done.40.refs_1_ = bf16[1,384,512]{2,1,0:T(8,128)(2,1)S(1)} collective-permute-done((bf16[1,384,512]{2,1,0:T(8,128)(2,1)}, bf16[1,384,512]{2,1,0:T(8,128)(2,1)S(1)}, u32[]{:S(2)}, u32[]{:S(2)}) %collective-permute-start.40) | collective-permute-done | bytes 393248 | tf_op jit(solution)/shard_map/ppermute | solution.py:23
  285.4 8.2 %shard_map.130 = (bf16[384,3072]{1,0:T(8,128)(2,1)}, bf16[384,3072]{1,0:T(8,128)(2,1)}, bf16[384,3072]{1,0:T(8,128)(2,1)}) custom-call(bf16[4,384,1664]{2,1,0:T(8,128)(2,1)} %shard_map.114.rows_ref, bf16[1664,1024]{1,0:T(8,128)(2,1)} %bitcast.28, s32[1,384]{1,0:T(1,128)} %doc_ref.11, s32[384,1]{1,0:T(8,128)} %copy.38.doc_column_ref, ...), custom_call_target="tpu_custom_call" | custom-call | flops 1409286144 | bytes 6127616 | tf_op jit(solution)/shard_map/pallas_call | solution.py:179
  299.6 8.2 %shard_map.131 = (bf16[384,3072]{1,0:T(8,128)(2,1)}, bf16[384,3072]{1,0:T(8,128)(2,1)}, bf16[384,3072]{1,0:T(8,128)(2,1)}) custom-call(bf16[4,384,1664]{2,1,0:T(8,128)(2,1)} %shard_map.114.rows_ref, bf16[1664,1024]{1,0:T(8,128)(2,1)} %bitcast.29, s32[1,384]{1,0:T(1,128)} %doc_ref.11, ...), custom_call_target="tpu_custom_call", output_to_operand_aliasing={{0}: (9, {}), {1}: (10, {}), {2}: (11, {})} | custom-call | flops 1409286144 | bytes 6127616 | tf_op jit(solution)/shard_map/pallas_call | solution.py:179
  314.5 12.7 %collective-permute-done.38.refs_1_ = bf16[1,384,512]{2,1,0:T(8,128)(2,1)S(1)} collective-permute-done((bf16[1,384,512]{2,1,0:T(8,128)(2,1)}, bf16[1,384,512]{2,1,0:T(8,128)(2,1)S(1)}, u32[]{:S(2)}, u32[]{:S(2)}) %collective-permute-start.38) | collective-permute-done | bytes 393248 | tf_op jit(solution)/shard_map/ppermute | solution.py:23
  328.0 8.2 %shard_map.132 = (bf16[384,3072]{1,0:T(8,128)(2,1)}, bf16[384,3072]{1,0:T(8,128)(2,1)}, bf16[384,3072]{1,0:T(8,128)(2,1)}) custom-call(bf16[4,384,1664]{2,1,0:T(8,128)(2,1)} %shard_map.114.rows_ref, bf16[1664,1024]{1,0:T(8,128)(2,1)} %bitcast.34, s32[1,384]{1,0:T(1,128)} %doc_ref.11, ...), custom_call_target="tpu_custom_call", output_to_operand_aliasing={{0}: (9, {}), {1}: (10, {}), {2}: (11, {})} | custom-call | flops 1409286144 | bytes 6127616 | tf_op jit(solution)/shard_map/pallas_call | solution.py:179
  336.9 8.2 %shard_map.133 = (bf16[384,3072]{1,0:T(8,128)(2,1)}, bf16[384,3072]{1,0:T(8,128)(2,1)}, bf16[384,3072]{1,0:T(8,128)(2,1)}) custom-call(bf16[4,384,1664]{2,1,0:T(8,128)(2,1)} %shard_map.114.rows_ref, bf16[1664,1024]{1,0:T(8,128)(2,1)} %bitcast.35, s32[1,384]{1,0:T(1,128)} %doc_ref.11, ...), custom_call_target="tpu_custom_call", output_to_operand_aliasing={{0}: (9, {}), {1}: (10, {}), {2}: (11, {})} | custom-call | flops 1409286144 | bytes 6127616 | tf_op jit(solution)/shard_map/pallas_call | solution.py:179
  346.0 8.2 %shard_map.134 = (bf16[384,3072]{1,0:T(8,128)(2,1)}, bf16[384,3072]{1,0:T(8,128)(2,1)}, bf16[384,3072]{1,0:T(8,128)(2,1)}) custom-call(bf16[4,384,1664]{2,1,0:T(8,128)(2,1)} %shard_map.114.rows_ref, bf16[1664,1024]{1,0:T(8,128)(2,1)} %bitcast.40, s32[1,384]{1,0:T(1,128)} %doc_ref.11, ...), custom_call_target="tpu_custom_call", output_to_operand_aliasing={{0}: (9, {}), {1}: (10, {}), {2}: (11, {})} | custom-call | flops 1409286144 | bytes 6127616 | tf_op jit(solution)/shard_map/pallas_call | solution.py:179
  354.9 8.2 %shard_map.135 = (bf16[384,3072]{1,0:T(8,128)(2,1)}, bf16[384,3072]{1,0:T(8,128)(2,1)}, bf16[384,3072]{1,0:T(8,128)(2,1)}) custom-call(bf16[4,384,1664]{2,1,0:T(8,128)(2,1)} %shard_map.114.rows_ref, bf16[1664,1024]{1,0:T(8,128)(2,1)} %bitcast.41, s32[1,384]{1,0:T(1,128)} %doc_ref.11, ...), custom_call_target="tpu_custom_call", output_to_operand_aliasing={{0}: (9, {}), {1}: (10, {}), {2}: (11, {})} | custom-call | flops 1409286144 | bytes 6127616 | tf_op jit(solution)/shard_map/pallas_call | solution.py:179
  (179 shorter events, 133.5 us)
Async XLA Ops:
  2.6 90.0 %collective-permute-start.26 = (bf16[416,1024]{1,0:T(8,128)(2,1)S(1)}, bf16[416,1024]{1,0:T(8,128)(2,1)S(1)}, u32[]{:S(2)}, u32[]{:S(2)}) collective-permute-start(bf16[416,1024]{1,0:T(8,128)(2,1)S(1)} %get-tuple-element.63.refs_0_), channel_id=1, source_target_pairs={{0,2},{1,3},{2,0},{3,1},{4,6},{5,7},{6,4},{7,5},{8,10},{9,11},{10,... | collective-permute-start | bytes 2555912 | tf_op jit(solution)/shard_map/ppermute | solution.py:23
  5.6 88.4 %collective-permute-start.27 = (bf16[416,1024]{1,0:T(8,128)(2,1)S(1)}, bf16[416,1024]{1,0:T(8,128)(2,1)}, u32[]{:S(2)}, u32[]{:S(2)}) collective-permute-start(bf16[416,1024]{1,0:T(8,128)(2,1)S(1)} %get-tuple-element.63.refs_0_), channel_id=1, source_target_pairs={{0,4},{1,5},{2,6},{3,7},{4,0},{5,1},{6,2},{7,3},{8,12},{9,13},{10,... | collective-permute-start | bytes 2555912 | tf_op jit(solution)/shard_map/ppermute | solution.py:23
  7.1 90.9 %collective-permute-start.28 = (bf16[416,1024]{1,0:T(8,128)(2,1)S(1)}, bf16[416,1024]{1,0:T(8,128)(2,1)}, u32[]{:S(2)}, u32[]{:S(2)}) collective-permute-start(bf16[416,1024]{1,0:T(8,128)(2,1)S(1)} %get-tuple-element.63.refs_0_), channel_id=1, source_target_pairs={{0,6},{1,7},{2,4},{3,5},{4,2},{5,3},{6,0},{7,1},{8,14},{9,15},{10,... | collective-permute-start | bytes 2555912 | tf_op jit(solution)/shard_map/ppermute | solution.py:23
  7.2 35.7 %collective-permute-start = (s32[1,384]{1,0:T(1,128)S(1)}, s32[1,384]{1,0:T(1,128)S(1)}, u32[]{:S(2)}, u32[]{:S(2)}) collective-permute-start(s32[1,384]{1,0:T(1,128)S(1)} %broadcast_in_dim.10), channel_id=1, source_target_pairs={{0,2},{1,3},{2,0},{3,1},{4,6},{5,7},{6,4},{7,5},{8,10},{9,11},{10,... | collective-permute-start | bytes 4616 | tf_op jit(solution)/shard_map/ppermute | solution.py:23
  13.0 74.1 %collective-permute-start.8 = (bf16[384,1664]{1,0:T(8,128)(2,1)}, bf16[384,1664]{1,0:T(8,128)(2,1)}, u32[]{:S(2)}, u32[]{:S(2)}) collective-permute-start(bf16[384,1664]{1,0:T(8,128)(2,1)} %get-tuple-element.61), channel_id=1, source_target_pairs={{0,8},{1,24},{2,10},{3,26},{4,12},{5,28},{6,14},{7,30},{8,0},{9,16... | collective-permute-start | bytes 3833864 | tf_op jit(solution)/shard_map/ppermute | solution.py:23
  58.6 35.8 %collective-permute-start.4 = (bf16[384,1664]{1,0:T(8,128)(2,1)}, bf16[384,1664]{1,0:T(8,128)(2,1)}, u32[]{:S(2)}, u32[]{:S(2)}) collective-permute-start(bf16[384,1664]{1,0:T(8,128)(2,1)} %get-tuple-element.62), channel_id=1, source_target_pairs={{0,0},{1,16},{2,2},{3,18},{4,4},{5,20},{6,6},{7,22},{8,8},{9,24},{... | collective-permute-start | bytes 3833864 | tf_op jit(solution)/shard_map/ppermute | solution.py:23
  98.1 37.2 %collective-permute-start.5 = (bf16[192,1664]{1,0:T(8,128)(2,1)}, bf16[192,1664]{1,0:T(8,128)(2,1)S(1)}, u32[]{:S(2)}, u32[]{:S(2)}) collective-permute-start(bf16[192,1664]{1,0:T(8,128)(2,1)} %get-tuple-element.33), channel_id=1, source_target_pairs={{0,2},{1,3},{2,0},{3,1},{4,6},{5,7},{6,4},{7,5},{8,10},{9,11},{10,... | collective-permute-start | bytes 1916936 | tf_op jit(solution)/shard_map/ppermute | solution.py:23
  108.4 35.0 %collective-permute-start.6 = (bf16[192,1664]{1,0:T(8,128)(2,1)}, bf16[192,1664]{1,0:T(8,128)(2,1)}, u32[]{:S(2)}, u32[]{:S(2)}) collective-permute-start(bf16[192,1664]{1,0:T(8,128)(2,1)} %get-tuple-element.34), channel_id=1, source_target_pairs={{0,4},{1,5},{2,6},{3,7},{4,0},{5,1},{6,2},{7,3},{8,12},{9,13},{10,... | collective-permute-start | bytes 1916936 | tf_op jit(solution)/shard_map/ppermute | solution.py:23
  151.8 37.2 %collective-permute-start.24 = (bf16[416,1024]{1,0:T(8,128)(2,1)S(1)}, bf16[416,1024]{1,0:T(8,128)(2,1)S(1)}, u32[]{:S(2)}, u32[]{:S(2)}) collective-permute-start(bf16[416,1024]{1,0:T(8,128)(2,1)S(1)} %get-tuple-element.41.refs_0_), channel_id=1, source_target_pairs={{0,4},{1,5},{2,6},{3,7},{4,0},{5,1},{6,2},{7,3},{8,12},{9,13},{10,... | collective-permute-start | bytes 2555912 | tf_op jit(solution)/shard_map/ppermute | solution.py:23
  152.9 39.0 %collective-permute-start.25 = (bf16[416,1024]{1,0:T(8,128)(2,1)S(1)}, bf16[416,1024]{1,0:T(8,128)(2,1)S(1)}, u32[]{:S(2)}, u32[]{:S(2)}) collective-permute-start(bf16[416,1024]{1,0:T(8,128)(2,1)S(1)} %get-tuple-element.41.refs_0_), channel_id=1, source_target_pairs={{0,6},{1,7},{2,4},{3,5},{4,2},{5,3},{6,0},{7,1},{8,14},{9,15},{10,... | collective-permute-start | bytes 2555912 | tf_op jit(solution)/shard_map/ppermute | solution.py:23
  167.7 34.1 %collective-permute-start.33 = (bf16[2,384,512]{2,1,0:T(8,128)(2,1)}, bf16[2,384,512]{2,1,0:T(8,128)(2,1)S(1)}, u32[]{:S(2)}, u32[]{:S(2)}) collective-permute-start(bf16[2,384,512]{2,1,0:T(8,128)(2,1)} %shard_map.124), channel_id=1, source_target_pairs={{0,8},{1,9},{2,10},{3,11},{4,12},{5,13},{6,14},{7,15},{8,0},{9,1},... | collective-permute-start | bytes 2359304 | tf_op jit(solution)/shard_map/ppermute | solution.py:23
  173.7 34.1 %collective-permute-start.29 = (bf16[2,384,512]{2,1,0:T(8,128)(2,1)}, bf16[2,384,512]{2,1,0:T(8,128)(2,1)S(1)}, u32[]{:S(2)}, u32[]{:S(2)}) collective-permute-start(bf16[2,384,512]{2,1,0:T(8,128)(2,1)} %shard_map.120), channel_id=1, source_target_pairs={{0,8},{1,9},{2,10},{3,11},{4,12},{5,13},{6,14},{7,15},{8,0},{9,1},... | collective-permute-start | bytes 2359304 | tf_op jit(solution)/shard_map/ppermute | solution.py:23
  174.1 35.0 %collective-permute-start.20 = (bf16[416,1024]{1,0:T(8,128)(2,1)S(1)}, bf16[416,1024]{1,0:T(8,128)(2,1)S(1)}, u32[]{:S(2)}, u32[]{:S(2)}) collective-permute-start(bf16[416,1024]{1,0:T(8,128)(2,1)S(1)} %get-tuple-element.40.refs_0_), channel_id=1, source_target_pairs={{0,2},{1,3},{2,0},{3,1},{4,6},{5,7},{6,4},{7,5},{8,10},{9,11},{10,... | collective-permute-start | bytes 2555912 | tf_op jit(solution)/shard_map/ppermute | solution.py:23
  191.9 35.8 %collective-permute-start.22 = (bf16[416,1024]{1,0:T(8,128)(2,1)S(1)}, bf16[416,1024]{1,0:T(8,128)(2,1)S(1)}, u32[]{:S(2)}, u32[]{:S(2)}) collective-permute-start(bf16[416,1024]{1,0:T(8,128)(2,1)S(1)} %get-tuple-element.40.refs_0_), channel_id=1, source_target_pairs={{0,6},{1,7},{2,4},{3,5},{4,2},{5,3},{6,0},{7,1},{8,14},{9,15},{10,... | collective-permute-start | bytes 2555912 | tf_op jit(solution)/shard_map/ppermute | solution.py:23
  201.8 35.1 %collective-permute-start.34 = (bf16[2,384,512]{2,1,0:T(8,128)(2,1)}, bf16[2,384,512]{2,1,0:T(8,128)(2,1)S(1)}, u32[]{:S(2)}, u32[]{:S(2)}) collective-permute-start(bf16[2,384,512]{2,1,0:T(8,128)(2,1)} %shard_map.123), channel_id=1, source_target_pairs={{0,8},{1,9},{2,10},{3,11},{4,12},{5,13},{6,14},{7,15},{8,0},{9,1},... | collective-permute-start | bytes 2359304 | tf_op jit(solution)/shard_map/ppermute | solution.py:23
  207.8 35.1 %collective-permute-start.30 = (bf16[2,384,512]{2,1,0:T(8,128)(2,1)}, bf16[2,384,512]{2,1,0:T(8,128)(2,1)S(1)}, u32[]{:S(2)}, u32[]{:S(2)}) collective-permute-start(bf16[2,384,512]{2,1,0:T(8,128)(2,1)} %shard_map.118), channel_id=1, source_target_pairs={{0,8},{1,9},{2,10},{3,11},{4,12},{5,13},{6,14},{7,15},{8,0},{9,1},... | collective-permute-start | bytes 2359304 | tf_op jit(solution)/shard_map/ppermute | solution.py:23
  236.9 56.8 %collective-permute-start.35 = (bf16[2,384,512]{2,1,0:T(8,128)(2,1)}, bf16[2,384,512]{2,1,0:T(8,128)(2,1)S(1)}, u32[]{:S(2)}, u32[]{:S(2)}) collective-permute-start(bf16[2,384,512]{2,1,0:T(8,128)(2,1)} %shard_map.122), channel_id=1, source_target_pairs={{0,8},{1,9},{2,10},{3,11},{4,12},{5,13},{6,14},{7,15},{8,0},{9,1},... | collective-permute-start | bytes 2359304 | tf_op jit(solution)/shard_map/ppermute | solution.py:23
  242.8 65.0 %collective-permute-start.31 = (bf16[2,384,512]{2,1,0:T(8,128)(2,1)}, bf16[2,384,512]{2,1,0:T(8,128)(2,1)S(1)}, u32[]{:S(2)}, u32[]{:S(2)}) collective-permute-start(bf16[2,384,512]{2,1,0:T(8,128)(2,1)} %shard_map.116), channel_id=1, source_target_pairs={{0,8},{1,9},{2,10},{3,11},{4,12},{5,13},{6,14},{7,15},{8,0},{9,1},... | collective-permute-start | bytes 2359304 | tf_op jit(solution)/shard_map/ppermute | solution.py:23
  246.8 35.2 %collective-permute-start.40 = (bf16[1,384,512]{2,1,0:T(8,128)(2,1)}, bf16[1,384,512]{2,1,0:T(8,128)(2,1)S(1)}, u32[]{:S(2)}, u32[]{:S(2)}) collective-permute-start(bf16[1,384,512]{2,1,0:T(8,128)(2,1)} %shard_map.129), channel_id=1, source_target_pairs={{0,16},{1,17},{2,18},{3,19},{4,20},{5,21},{6,22},{7,23},{8,24},{9,... | collective-permute-start | bytes 1179656 | tf_op jit(solution)/shard_map/ppermute | solution.py:23
  251.1 47.7 %collective-permute-start.39 = (bf16[1,384,512]{2,1,0:T(8,128)(2,1)}, bf16[1,384,512]{2,1,0:T(8,128)(2,1)S(1)}, u32[]{:S(2)}, u32[]{:S(2)}) collective-permute-start(bf16[1,384,512]{2,1,0:T(8,128)(2,1)} %shard_map.128), channel_id=1, source_target_pairs={{0,16},{1,17},{2,18},{3,19},{4,20},{5,21},{6,22},{7,23},{8,24},{9,... | collective-permute-start | bytes 1179656 | tf_op jit(solution)/shard_map/ppermute | solution.py:23
  257.7 69.6 %collective-permute-start.38 = (bf16[1,384,512]{2,1,0:T(8,128)(2,1)}, bf16[1,384,512]{2,1,0:T(8,128)(2,1)S(1)}, u32[]{:S(2)}, u32[]{:S(2)}) collective-permute-start(bf16[1,384,512]{2,1,0:T(8,128)(2,1)} %shard_map.127), channel_id=1, source_target_pairs={{0,16},{1,17},{2,18},{3,19},{4,20},{5,21},{6,22},{7,23},{8,24},{9,... | collective-permute-start | bytes 1179656 | tf_op jit(solution)/shard_map/ppermute | solution.py:23
  282.1 54.1 %collective-permute-start.37 = (bf16[1,384,512]{2,1,0:T(8,128)(2,1)}, bf16[1,384,512]{2,1,0:T(8,128)(2,1)S(1)}, u32[]{:S(2)}, u32[]{:S(2)}) collective-permute-start(bf16[1,384,512]{2,1,0:T(8,128)(2,1)} %shard_map.126), channel_id=1, source_target_pairs={{0,16},{1,17},{2,18},{3,19},{4,20},{5,21},{6,22},{7,23},{8,24},{9,... | collective-permute-start | bytes 1179656 | tf_op jit(solution)/shard_map/ppermute | solution.py:23
  298.1 47.1 %collective-permute-start.36 = (bf16[1,384,512]{2,1,0:T(8,128)(2,1)}, bf16[1,384,512]{2,1,0:T(8,128)(2,1)S(1)}, u32[]{:S(2)}, u32[]{:S(2)}) collective-permute-start(bf16[1,384,512]{2,1,0:T(8,128)(2,1)} %shard_map.125), channel_id=1, source_target_pairs={{0,16},{1,17},{2,18},{3,19},{4,20},{5,21},{6,22},{7,23},{8,24},{9,... | collective-permute-start | bytes 1179656 | tf_op jit(solution)/shard_map/ppermute | solution.py:23
  312.3 41.9 %collective-permute-start.32 = (bf16[1,384,512]{2,1,0:T(8,128)(2,1)}, bf16[1,384,512]{2,1,0:T(8,128)(2,1)S(1)}, u32[]{:S(2)}, u32[]{:S(2)}) collective-permute-start(bf16[1,384,512]{2,1,0:T(8,128)(2,1)} %shard_map.121), channel_id=1, source_target_pairs={{0,16},{1,17},{2,18},{3,19},{4,20},{5,21},{6,22},{7,23},{8,24},{9,... | collective-permute-start | bytes 1179656 | tf_op jit(solution)/shard_map/ppermute | solution.py:23
  (51 other events, 935.1 us)

commit v2 on v0

v2 whole, which is shorter than its diff:
```python
import functools
import math

import jax
import jax.numpy as jnp
from jax import lax
from jax.experimental import pallas as pl
from jax.experimental.pallas import tpu as pltpu
from jax.sharding import PartitionSpec as P

HS = 128
INNER = 4
AXES = ("peer", "tp")
ROW_PARTS = 3
COST = pl.CostEstimate(flops=1000, bytes_accessed=1000, transcendentals=0)
PARAMS = pltpu.CompilerParams(vmem_limit_bytes=56 * 1024 * 1024)


def swap(array, peers, cores, move):
    pairs = []
    for peer in range(peers):
        for core in range(cores):
            to_peer, to_core = move(peer, core)
            pairs.append((peer * cores + core, to_peer * cores + to_core))
    return lax.ppermute(array, AXES, pairs)


def after(array, *others):
    return lax.optimization_barrier((array,) + others)[0]


def route_kernel(shift, own_ref, known_ref, position_ref, slots_ref):
    plane, inner, peers = own_ref[0], own_ref[1], slots_ref.shape[1] * INNER
    tok_count = known_ref.shape[1]
    sources, planes, room = slots_ref.shape
    span = position_ref.shape[0]
    rows = [known_ref[n : n + 1, :].astype(jnp.int32) for n in range(sources)]
    peer_at = lax.broadcasted_iota(jnp.int32, (peers, tok_count), 0)
    named = [(peer_at == (row >> shift)).astype(jnp.float32) for row in rows]
    before = (
        lax.broadcasted_iota(jnp.int32, (tok_count, tok_count), 0)
        < lax.broadcasted_iota(jnp.int32, (tok_count, tok_count), 1)
    ).astype(jnp.float32)
    counts = jnp.dot(
        jnp.concatenate(named, axis=0).astype(jnp.bfloat16),
        before.astype(jnp.bfloat16),
        preferred_element_type=jnp.float32,
    )
    group_at = lax.broadcasted_iota(jnp.int32, (max(planes, 8), tok_count), 0)
    room_at = lax.broadcasted_iota(jnp.int32, (room, tok_count), 0)
    for n, row in enumerate(rows):
        target, slot = row >> shift, (row & ((1 << shift) - 1)) + 1
        within = jnp.sum(named[n] * counts[n * peers : (n + 1) * peers], axis=0, keepdims=True).astype(jnp.int32)
        group, place_in = (target // INNER) ^ plane, (target % INNER) ^ inner
        if n < span:
            position_ref[n : n + 1, :] = (place_in * planes + group) * room + within
        here = (group_at == group) & (place_in == 0)
        high = jnp.where(here, (slot >> 4).astype(jnp.float32), 0.0)
        low = jnp.where(here, (slot & 15).astype(jnp.float32), 0.0)
        both = jnp.concatenate([high, low], axis=0).astype(jnp.bfloat16)
        filled = (room_at == within).astype(jnp.float32).astype(jnp.bfloat16)
        found = lax.dot_general(both, filled, (((1,), (1,)), ((), ())), preferred_element_type=jnp.float32)
        half = group_at.shape[0]
        value = found[:half] * 16.0 + found[half:] - 1.0
        slots_ref[n] = value[:planes].astype(jnp.int32)


def route(own, known, shift, planes, span, room):
    sources, tok_count = known.shape
    position, slots = pl.pallas_call(
        functools.partial(route_kernel, shift),
        in_specs=[pl.BlockSpec(memory_space=pltpu.SMEM), pl.BlockSpec((sources, tok_count), lambda: (0, 0))],
        out_shape=[
            jax.ShapeDtypeStruct((span, tok_count), jnp.int32),
            jax.ShapeDtypeStruct((sources, planes, room), jnp.int32),
        ],
        compiler_params=PARAMS,
        cost_estimate=COST,
    )(own, known)
    return position, jnp.transpose(slots, (1, 0, 2)).reshape(planes, 1, sources * room)


def pack_kernel(sources, position_ref, scale_ref, *refs):
    rows_refs, out_refs = refs[:sources], refs[sources:]
    count = out_refs[0].shape[1]
    for r, rows_ref in enumerate(rows_refs):
        rows = rows_ref[...]
        for k, out_ref in enumerate(out_refs):
            places = lax.broadcasted_iota(jnp.int32, (count, rows.shape[0]), 0) + k * count
            chosen = (places == position_ref[r : r + 1, :]).astype(jnp.float32)
            scale = jnp.sum(chosen * scale_ref[r : r + 1, :], axis=1, keepdims=True)
            picked = jnp.dot(chosen.astype(jnp.bfloat16), rows, preferred_element_type=jnp.float32)
            out_ref[r] = (picked * scale).astype(jnp.bfloat16)


def pack(position, scale, rows, count):
    sources, width = len(rows), rows[0].shape[1]
    return pl.pallas_call(
        functools.partial(pack_kernel, sources),
        out_shape=[jax.ShapeDtypeStruct((sources, count, width), jnp.bfloat16)] * INNER,
        compiler_params=PARAMS,
        cost_estimate=COST,
    )(position, scale, *rows)


def place_kernel(slots_ref, *refs):
    out_ref = refs[-1]
    rows = jnp.concatenate([ref[r, 0] for ref in refs[:-1] for r in range(ref.shape[0])], axis=0)
    tokens = lax.broadcasted_iota(jnp.int32, (out_ref.shape[1], rows.shape[0]), 0)
    chosen = (tokens == slots_ref[0]).astype(jnp.float32).astype(jnp.bfloat16)
    out_ref[0] = jnp.dot(chosen, rows, preferred_element_type=jnp.float32).astype(jnp.bfloat16)


def place(slots, pieces, tok_count):
    sources, groups, room, width = pieces[0].shape
    total = slots.shape[2]
    return pl.pallas_call(
        place_kernel,
        grid=(groups,),
        in_specs=[pl.BlockSpec((1, 1, total), lambda t: (t, 0, 0))]
        + [pl.BlockSpec((sources, 1, room, width), lambda t: (0, t, 0, 0))] * len(pieces),
        out_specs=pl.BlockSpec((1, tok_count, width), lambda t: (t, 0, 0)),
        out_shape=jax.ShapeDtypeStruct((groups, tok_count, width), jnp.bfloat16),
        compiler_params=PARAMS,
        cost_estimate=COST,
    )(slots, *pieces)


def product_kernel(n_rows, n_pieces, own_ref, *refs):
    leave_ref, keep_ref, weight_ref = refs[-3:]
    m, half = pl.program_id(0), pl.num_programs(0) // 2

    @pl.when(m == 0)
    def _():
        for k, ref in enumerate(refs[n_rows : n_rows + n_pieces]):
            depth = ref.shape[0]
            if n_pieces == 1:
                weight_ref[...] = ref[...]
            else:
                at = pl.multiple_of((k ^ own_ref[1]) * depth, 16)
                weight_ref[pl.ds(at, depth), :] = ref[...]

    total, start = None, 0
    for ref in refs[:n_rows]:
        stop = start + ref.shape[2]
        term = jnp.dot(ref[0], weight_ref[start:stop, :], preferred_element_type=jnp.float32)
        total = term if total is None else total + term
        start = stop

    @pl.when(m < half)
    def _():
        leave_ref[0] = total.astype(jnp.bfloat16)

    @pl.when(m >= half)
    def _():
        keep_ref[0] = total


def product(own, rows, pieces, block, columns):
    groups, tok_count = rows[0].shape[:2]
    width, half = sum(part.shape[2] for part in rows), groups // 2
    depth = pieces[0].shape[0]
    if depth % 16:
        places = jnp.arange(len(pieces), dtype=jnp.int32) ^ own[1]
        pieces = [jnp.stack(pieces)[places].reshape(width, -1)]
        depth = width
    in_specs = [pl.BlockSpec(memory_space=pltpu.SMEM)]
    in_specs += [
        pl.BlockSpec((1, tok_count, part.shape[2]), lambda m: (jnp.where(m < half, 2 * m + 1, 2 * (m - half)), 0, 0))
        for part in rows
    ]
    in_specs += [pl.BlockSpec((depth, columns), lambda m: (0, block))] * len(pieces)
    out_block = (1, tok_count, columns)
    return pl.pallas_call(
        functools.partial(product_kernel, len(rows), len(pieces)),
        grid=(groups,),
        in_specs=in_specs,
        out_specs=[
            pl.BlockSpec(out_block, lambda m: (jnp.minimum(m, half - 1), 0, 0)),
            pl.BlockSpec(out_block, lambda m: (jnp.maximum(m - half, 0), 0, 0)),
        ],
        out_shape=[
            jax.ShapeDtypeStruct((half, tok_count, columns), jnp.bfloat16),
            jax.ShapeDtypeStruct((half, tok_count, columns), jnp.float32),
        ],
        scratch_shapes=[pltpu.VMEM((width, columns), jnp.bfloat16)],
        compiler_params=PARAMS,
        cost_estimate=COST,
    )(own, *rows, *pieces)


def attend_kernel(heads, n_parts, *refs):
    parts = refs[:n_parts]
    doc_ref, doc_column_ref, q_ref, k_ref, v_ref = refs[n_parts : n_parts + 5]
    dq_ref, dk_ref, dv_ref = refs[-3:]
    count = q_ref.shape[0]
    factor = 1.0 / math.sqrt(HS)
    across = (((1,), (1,)), ((), ()))
    down = (((0,), (0,)), ((), ()))
    key_at = lax.broadcasted_iota(jnp.int32, (count, count), 0)
    query_at = lax.broadcasted_iota(jnp.int32, (count, count), 1)
    allowed = (doc_column_ref[...] == doc_ref[...]) & (key_at <= query_at)
    for h in range(heads):
        at = slice(h * HS, (h + 1) * HS)
        total = parts[0][0, :, at]
        for ref in parts[1:]:
            total = total + ref[0, :, at].astype(jnp.float32)
        grad = total.astype(jnp.bfloat16)
        q, k, v = q_ref[:, at], k_ref[:, at], v_ref[:, at]
        scores = lax.dot_general(k, q, across, preferred_element_type=jnp.float32) * factor
        scores = jnp.where(allowed, scores, -1e30)
        raised = jnp.exp(scores - jnp.max(scores, axis=0, keepdims=True))
        probs = raised * (1.0 / jnp.sum(raised, axis=0, keepdims=True))
        grad_p = lax.dot_general(v, grad, across, preferred_element_type=jnp.float32)
        delta = jnp.sum(probs * grad_p, axis=0, keepdims=True)
        grad_s = (probs * (grad_p - delta)).astype(jnp.bfloat16)
        probs_low = probs.astype(jnp.bfloat16)
        dv_ref[:, at] = jnp.dot(probs_low, grad, preferred_element_type=jnp.float32).astype(jnp.bfloat16)
        dk = jnp.dot(grad_s, q, preferred_element_type=jnp.float32) * factor
        dk_ref[:, at] = dk.astype(jnp.bfloat16)
        dq = lax.dot_general(grad_s, k, down, preferred_element_type=jnp.float32) * factor
        dq_ref[:, at] = dq.astype(jnp.bfloat16)


def attend(parts, first_head, heads, doc, query, key, value, old):
    tok_count, features = query.shape
    columns = heads * HS
    block = first_head // heads
    chunk_spec = pl.BlockSpec((tok_count, columns), lambda i: (0, block))
    in_specs = [pl.BlockSpec((1, tok_count, columns), lambda i: (0, 0, 0))] * len(parts)
    in_specs += [
        pl.BlockSpec((1, tok_count), lambda i: (0, 0)),
        pl.BlockSpec((tok_count, 1), lambda i: (0, 0)),
        chunk_spec,
        chunk_spec,
        chunk_spec,
    ]
    in_specs += [pl.BlockSpec(memory_space=pl.ANY)] * len(old)
    base = len(parts) + 5
    return pl.pallas_call(
        functools.partial(attend_kernel, heads, len(parts)),
        grid=(1,),
        in_specs=in_specs,
        out_specs=[chunk_spec] * 3,
        out_shape=[jax.ShapeDtypeStruct((tok_count, features), jnp.bfloat16)] * 3,
        input_output_aliases={base + n: n for n in range(len(old))},
        compiler_params=PARAMS,
        cost_estimate=COST,
    )(*parts, doc, doc.reshape(tok_count, 1), query, key, value, *old)


def cut(total, parts):
    tiles = total // 128
    sizes = [tiles // parts * 128 + (128 if n < tiles % parts else 0) for n in range(parts)]
    sizes[-1] += total - sum(sizes)
    return sizes


def shards(
    grad_blocks,
    row_scale,
    dest_peer,
    dest_slot,
    doc_ids,
    query_rows,
    key_rows,
    value_rows,
    out_weight,
):
    tok_count, width_part = grad_blocks.shape
    peers, cores = lax.axis_size("peer"), lax.axis_size("tp")
    planes = peers // INNER
    span = planes // cores
    width = width_part // span
    capacity = 2 * tok_count // peers
    room = -(-capacity // 16) * 16
    levels = planes.bit_length() - 1
    me, core = lax.axis_index("peer"), lax.axis_index("tp")
    plane, inner = me // INNER, me % INNER
    own = jnp.stack([plane, inner]).astype(jnp.int32)
    send = functools.partial(swap, peers=peers, cores=cores)

    def to_plane(array, r):
        def move(p, c):
            o, i = p // INNER, p % INNER
            return (c * span + ((o % span) ^ r)) * INNER + i, o // span

        return send(array, move=move)

    shift = (tok_count - 1).bit_length()
    known = ((dest_peer[:, 0] << shift) + dest_slot).astype(jnp.float32)
    known = jnp.stack([known, row_scale])
    near = jnp.stack([to_plane(known, r) for r in range(span)])
    known, scale = near[:, 0], near[:, 1]
    for step in (1, 2):
        known = jnp.concatenate([known, send(known, move=lambda p, c: (p ^ step, c))], axis=0)
    position, slots = route(own, known, shift, planes, span, room)

    widths = cut(width, ROW_PARTS)
    plane_rows, start = [], 0
    for size in widths:
        parts = []
        for r in range(span):
            at = ((plane % span) ^ r) * width + start
            part = lax.dynamic_slice(grad_blocks, (0, at), (tok_count, size))
            part = after(part, near)
            parts.append(to_plane(part, r))
        plane_rows.append(parts)
        start += size

    weight = out_weight.T
    n_heads = weight.shape[1] // HS
    sixth = n_heads // 6
    heads = [sixth] * 5 + ([sixth // 2] * 2 if sixth % 2 == 0 else [sixth])
    firsts = [sum(heads[:n]) for n in range(len(heads))]
    group_of = [0, 0, 0] + [1] * (len(heads) - 3)
    group_first = [0, 3 * sixth, n_heads]

    def gather_weight(g, hold):
        part = weight[:, group_first[g] * HS : group_first[g + 1] * HS]
        if hold is not None:
            part = after(part, hold)
        members = [[n * INNER + k for k in range(INNER)] for n in range(planes)]
        return [lax.all_gather(part, "peer", axis=0, tiled=True, axis_index_groups=members)]

    weights = [gather_weight(0, None)]

    rows, last, packed = [], None, None
    for parts in plane_rows:
        if packed is not None:
            parts = [after(parts[0], packed[0])] + parts[1:]
        packed = pack(position, scale, parts, planes * room)
        pieces = [packed[0]] + [send(packed[k], move=lambda p, c: (p ^ k, c)) for k in range(1, INNER)]
        if last is not None:
            pieces[0] = after(pieces[0], last)
        summed = place(slots, [one.reshape(span, planes, room, one.shape[2]) for one in pieces], tok_count)
        last = summed
        step = 1
        while step < cores:
            other = send(summed, move=lambda p, c: (p, c ^ step))
            summed = (summed.astype(jnp.float32) + other.astype(jnp.float32)).astype(jnp.bfloat16)
            step *= 2
        rows.append(summed)

    weights.append(gather_weight(1, last))

    count = len(heads)
    last = rows[-1]
    leaving, arrived, kept = {}, {}, {}
    old = []

    def multiply(n):
        nonlocal last
        g = group_of[n]
        pieces = weights[g]
        first = (firsts[n] - group_first[g]) // heads[n]
        leaving[n], kept[n] = product(own, rows, [after(pieces[0], last)] + pieces[1:], first, heads[n] * HS)
        last = leaving[n]

    def launch(n, level, part):
        arrived.setdefault(n, []).append(send(part, move=lambda p, c: (p ^ (INNER << level), c)))

    def pass_on(n, level, *hold):
        nonlocal last
        part = after(kept[n], last, *hold)[1 << (level - 1) :: 1 << level]
        for j, one in enumerate(arrived[n]):
            part = part + one[1 << (level - j - 1) :: 1 << (level - j)].astype(jnp.float32)
        last = part.astype(jnp.bfloat16)
        launch(n, level, last)

    def finish(n):
        nonlocal old, last
        parts = [after(kept[n], last)] + arrived[n]
        old = attend(parts, firsts[n], heads[n], doc_ids, query_rows, key_rows, value_rows, old)
        last = old[0]

    for n in range(3):
        multiply(n)
        if n < 2:
            launch(n, 0, leaving[n])
    for n in range(count):
        for level in range(1, levels):
            pass_on(n, level, *(arrived[n - 1][-1:] if n else []))
        if n + 2 < count:
            launch(n + 2, 0, after(leaving[n + 2], last))
        if n + 3 < count:
            multiply(n + 3)
        if n >= 1:
            finish(n - 1)
    finish(count - 1)
    return tuple(old)


def solution(mesh):
    return jax.shard_map(
        shards,
        mesh=mesh,
        in_specs=(
            P("peer", "tp"),
            P("peer"),
            P("peer", None),
            P("peer"),
            P("peer", None),
            P("peer", "tp"),
            P("peer", "tp"),
            P("peer", "tp"),
            P("tp", "peer"),
        ),
        out_specs=(P("peer", "tp"), P("peer", "tp"), P("peer", "tp")),
        check_vma=False,
    )
```

time: 833 us -> 327 us (0.39)
  waiting for transfers between devices: 641 us -> 118 us
  Pallas kernels: 0 us -> 107 us
  matrix products: 75.1 us -> 0 us
  starting transfers between devices: 15.7 us -> 67.7 us
  other arithmetic: 49.3 us -> 10.2 us
  local copies, waits for them, and re-layouts: 31.4 us -> 8.69 us
    all_gather x2, waiting for transfers between devices: 449 us -> 16.2 us  [gather_weight(): lax.all_gather(part, 'peer', axis=0, tiled=True, axis_index_groups=members)]
    all_to_all x2 -> x0, waiting for transfers between devices: 191 us -> none  [the longest x1 191 us: shards(): lax.all_to_all(buffer_rows.reshape(peer_count, capacity, width_part), 'pe...]
    pallas_call x0 -> x21, Pallas kernels: none -> 107 us  [the longest x7 48.9 us: product(): pl.pallas_call(functools.partial(product_kernel, len(rows), len(pieces)),...]
    ppermute x0 -> x36, waiting for transfers between devices: none -> 102 us  [swap(): return lax.ppermute(array, AXES, pairs)]
    dot_general x7 -> x0, matrix products: 75.1 us -> none  [the longest x1 23.6 us: shards(): lax.dot_general(full_rows, lax.all_gather(out_weight, 'peer', axis=1, til...]
    ppermute x0 -> x36, starting transfers between devices: none -> 67.7 us  [swap(): return lax.ppermute(array, AXES, pairs)]
    scatter-add x1 -> x0, other arithmetic: 24.5 us -> none  [shards(): jnp.zeros((tok_count, width_part), jnp.float32).at[landing]]
    all_to_all x2 -> x0, starting transfers between devices: 15.3 us -> none  [the longest x1 8.31 us: shards(): lax.all_to_all(buffer_slots.reshape(peer_count, capacity), 'peer', split_...]
  transfers between devices with their start and end apart: 4 -> 38, of which waited for: 3 -> 22; matrix products, arithmetic and copies ran while one was open for 5% -> 4% of each run, Pallas kernels for 0% -> 32%
where the time goes in v2:
time: 327 us; the launch traced here: 326 us
  waiting for transfers between devices  118 us (36%)
  Pallas kernels  107 us (33%)
  starting transfers between devices  67.7 us (21%)
  between operations  14.4 us (4%)
  other arithmetic  10.2 us (3%)
  local copies, waits for them, and re-layouts  8.69 us (3%)
    ppermute x36, waiting for transfers between devices, swap(): return lax.ppermute(array, AXES, pairs)  102 us
    ppermute x36, starting transfers between devices, swap(): return lax.ppermute(array, AXES, pairs)  67.7 us
    pallas_call x7, Pallas kernels, product(): pl.pallas_call(functools.partial(product_kernel, len(rows), len(pieces)),...  48.9 us
    pallas_call x7, Pallas kernels, attend(): pl.pallas_call(functools.partial(attend_kernel, heads, len(parts)), grid=...  33.6 us
    all_gather x2, waiting for transfers between devices, gather_weight(): lax.all_gather(part, 'peer', axis=0, tiled=True, axis_index_groups=members)  16.2 us
    pallas_call x3, Pallas kernels, place(): pl.pallas_call(place_kernel, grid=(groups,), in_specs=[pl.BlockSpec((1, 1...  13.5 us
    pallas_call x3, Pallas kernels, pack(): pl.pallas_call(functools.partial(pack_kernel, sources), out_shape=[jax.Sh...  9.34 us
  transfers between devices with their start and end apart: 38, of which 22 were waited for; matrix products, arithmetic and copies ran while one was open for 4% of the time, Pallas kernels for 32%

profile of v2, /device:TPU:0, one launch (start us, length us, event | category | flops | bytes accessed | tf_op | source)
XLA Modules:
  0.0 326.1 jit_solution(13744406451626414290)
XLA Ops:
  43.3 6.4 %collective-permute-done.17.refs_1_ = bf16[384,512]{1,0:T(8,128)(2,1)S(1)} collective-permute-done((bf16[384,512]{1,0:T(8,128)(2,1)}, bf16[384,512]{1,0:T(8,128)(2,1)S(1)}, u32[]{:S(2)}, u32[]{:S(2)}) %collective-permute-start.17) | collective-permute-done | bytes 393248 | tf_op jit(solution)/shard_map/ppermute | solution.py:25
  51.3 20.9 %collective-permute-done.12 = bf16[2,192,512]{2,1,0:T(8,128)(2,1)S(1)} collective-permute-done((bf16[2,192,512]{2,1,0:T(8,128)(2,1)}, bf16[2,192,512]{2,1,0:T(8,128)(2,1)S(1)}, u32[]{:S(2)}, u32[]{:S(2)}) %collective-permute-start.12) | collective-permute-done | bytes 393248 | tf_op jit(solution)/shard_map/ppermute | solution.py:25
  80.7 4.8 %shard_map.114 = bf16[4,384,640]{2,1,0:T(8,128)(2,1)} custom-call(s32[4,1,384]{2,1,0:T(1,128)} %reshape.56.slots_ref, bf16[2,4,48,640]{3,2,1,0:T(8,128)(2,1)} %bitcast.23, bf16[2,4,48,640]{3,2,1,0:T(8,128)(2,1)} %bitcast.24, bf16[2,4,48,640]{3,2,1,0:T(8,128)(2,1)} %bitcast.25, bf16[2,4,48,640]{3,2,1,0:T(8,128)(2,1)} %bitcast.26), custom_call_target="tpu_custom_call" | custom-call | flops 1000 | bytes 1000 | tf_op jit(solution)/shard_map/pallas_call | solution.py:117
  85.5 8.2 %collective-permute-done.14 = bf16[2,192,512]{2,1,0:T(8,128)(2,1)S(1)} collective-permute-done((bf16[2,192,512]{2,1,0:T(8,128)(2,1)}, bf16[2,192,512]{2,1,0:T(8,128)(2,1)S(1)}, u32[]{:S(2)}, u32[]{:S(2)}) %collective-permute-start.14) | collective-permute-done | bytes 393248 | tf_op jit(solution)/shard_map/ppermute | solution.py:25
  98.8 6.4 %collective-permute-done.18 = bf16[2,192,512]{2,1,0:T(8,128)(2,1)} collective-permute-done((bf16[2,192,512]{2,1,0:T(8,128)(2,1)}, bf16[2,192,512]{2,1,0:T(8,128)(2,1)}, u32[]{:S(2)}, u32[]{:S(2)}) %collective-permute-start.18) | collective-permute-done | bytes 393248 | tf_op jit(solution)/shard_map/ppermute | solution.py:25
  105.2 6.6 %collective-permute-done.20 = bf16[2,192,512]{2,1,0:T(8,128)(2,1)} collective-permute-done((bf16[2,192,512]{2,1,0:T(8,128)(2,1)}, bf16[2,192,512]{2,1,0:T(8,128)(2,1)}, u32[]{:S(2)}, u32[]{:S(2)}) %collective-permute-start.20) | collective-permute-done | bytes 393248 | tf_op jit(solution)/shard_map/ppermute | solution.py:25
  116.1 11.3 %collective-permute-start.21 = (bf16[4,384,512]{2,1,0:T(8,128)(2,1)}, bf16[4,384,512]{2,1,0:T(8,128)(2,1)S(1)}, u32[]{:S(2)}, u32[]{:S(2)}) collective-permute-start(bf16[4,384,512]{2,1,0:T(8,128)(2,1)} %shard_map.118), channel_id=1, source_target_pairs={{0,1},{1,0},{2,3},{3,2},{4,5},{5,4},{6,7},{7,6},{8,9},{9,8},{10,11... | collective-permute-start | bytes 4718600 | tf_op jit(solution)/shard_map/ppermute | solution.py:25
  139.1 7.7 %shard_map.119 = (bf16[2,384,512]{2,1,0:T(8,128)(2,1)}, f32[2,384,512]{2,1,0:T(8,128)}) custom-call(s32[2]{0:T(128)} %pad_add_fusion.own_ref, bf16[4,384,640]{2,1,0:T(8,128)(2,1)} %add_convert_fusion.refs_0_, bf16[4,384,512]{2,1,0:T(8,128)(2,1)} %add_convert_fusion.2.refs_1_, bf16[4,384,512]{2,1,0:T(8,128)(2,1)} %add_convert_fusion.1.refs_2_, ...), custom_call_target="tpu_custom_call" | custom-call | flops 1000 | bytes 1000 | tf_op jit(solution)/shard_map/pallas_call | solution.py:174
  150.8 7.4 %shard_map.120 = (bf16[2,384,512]{2,1,0:T(8,128)(2,1)}, f32[2,384,512]{2,1,0:T(8,128)}) custom-call(s32[2]{0:T(128)} %pad_add_fusion.own_ref, bf16[4,384,640]{2,1,0:T(8,128)(2,1)} %add_convert_fusion.refs_0_, bf16[4,384,512]{2,1,0:T(8,128)(2,1)} %add_convert_fusion.2.refs_1_, bf16[4,384,512]{2,1,0:T(8,128)(2,1)} %add_convert_fusion.1.refs_2_, ...), custom_call_target="tpu_custom_call" | custom-call | flops 1000 | bytes 1000 | tf_op jit(solution)/shard_map/pallas_call | solution.py:174
  158.3 7.6 %shard_map.121 = (bf16[2,384,512]{2,1,0:T(8,128)(2,1)}, f32[2,384,512]{2,1,0:T(8,128)}) custom-call(s32[2]{0:T(128)} %pad_add_fusion.own_ref, bf16[4,384,640]{2,1,0:T(8,128)(2,1)} %add_convert_fusion.refs_0_, bf16[4,384,512]{2,1,0:T(8,128)(2,1)} %add_convert_fusion.2.refs_1_, bf16[4,384,512]{2,1,0:T(8,128)(2,1)} %add_convert_fusion.1.refs_2_, ...), custom_call_target="tpu_custom_call" | custom-call | flops 1000 | bytes 1000 | tf_op jit(solution)/shard_map/pallas_call | solution.py:174
  174.4 16.2 %all-gather.3.cloned.1.call-done.refs_3_ = bf16[1664,1536]{1,0:T(8,128)(2,1)} async-done(((bf16[416,1536]{1,0:T(8,128)(2,1)}), bf16[1664,1536]{1,0:T(8,128)(2,1)}) %all-gather.3.cloned.1.call-update) | async-done | bytes 5111824 | tf_op jit(solution)/shard_map/all_gather | solution.py:324
  190.6 7.4 %shard_map.122 = (bf16[2,384,512]{2,1,0:T(8,128)(2,1)}, f32[2,384,512]{2,1,0:T(8,128)}) custom-call(s32[2]{0:T(128)} %pad_add_fusion.own_ref, bf16[4,384,640]{2,1,0:T(8,128)(2,1)} %add_convert_fusion.refs_0_, bf16[4,384,512]{2,1,0:T(8,128)(2,1)} %add_convert_fusion.2.refs_1_, bf16[4,384,512]{2,1,0:T(8,128)(2,1)} %add_convert_fusion.1.refs_2_, ...), custom_call_target="tpu_custom_call" | custom-call | flops 1000 | bytes 1000 | tf_op jit(solution)/shard_map/pallas_call | solution.py:174
  203.9 7.4 %shard_map.123 = (bf16[2,384,512]{2,1,0:T(8,128)(2,1)}, f32[2,384,512]{2,1,0:T(8,128)}) custom-call(s32[2]{0:T(128)} %pad_add_fusion.own_ref, bf16[4,384,640]{2,1,0:T(8,128)(2,1)} %add_convert_fusion.refs_0_, bf16[4,384,512]{2,1,0:T(8,128)(2,1)} %add_convert_fusion.2.refs_1_, bf16[4,384,512]{2,1,0:T(8,128)(2,1)} %add_convert_fusion.1.refs_2_, ...), custom_call_target="tpu_custom_call" | custom-call | flops 1000 | bytes 1000 | tf_op jit(solution)/shard_map/pallas_call | solution.py:174
  211.3 5.3 %shard_map.124 = (bf16[384,3072]{1,0:T(8,128)(2,1)}, bf16[384,3072]{1,0:T(8,128)(2,1)}, bf16[384,3072]{1,0:T(8,128)(2,1)}) custom-call(f32[2,384,512]{2,1,0:T(8,128)} %get-tuple-element.127.refs_0_, bf16[2,384,512]{2,1,0:T(8,128)(2,1)} %copy-done.13, bf16[1,384,512]{2,1,0:T(8,128)(2,1)} %copy-done.28, s32[1,384]{1,0:T(1,128)} %refs_3_.13, ...), custom_call_target="tpu_custom_call" | custom-call | flops 1000 | bytes 1000 | tf_op jit(solution)/shard_map/pallas_call | solution.py:240
  224.4 5.7 %shard_map.125 = (bf16[2,384,256]{2,1,0:T(8,128)(2,1)}, f32[2,384,256]{2,1,0:T(8,128)}) custom-call(s32[2]{0:T(128)} %pad_add_fusion.own_ref, bf16[4,384,640]{2,1,0:T(8,128)(2,1)} %add_convert_fusion.refs_0_, bf16[4,384,512]{2,1,0:T(8,128)(2,1)} %add_convert_fusion.2.refs_1_, bf16[4,384,512]{2,1,0:T(8,128)(2,1)} %add_convert_fusion.1.refs_2_, ...), custom_call_target="tpu_custom_call" | custom-call | flops 1000 | bytes 1000 | tf_op jit(solution)/shard_map/pallas_call | solution.py:174
  230.1 5.3 %shard_map.126 = (bf16[384,3072]{1,0:T(8,128)(2,1)}, bf16[384,3072]{1,0:T(8,128)(2,1)}, bf16[384,3072]{1,0:T(8,128)(2,1)}) custom-call(f32[2,384,512]{2,1,0:T(8,128)} %get-tuple-element.133.refs_0_, bf16[2,384,512]{2,1,0:T(8,128)(2,1)} %collective-permute-done.24.refs_1_, ...), custom_call_target="tpu_custom_call", output_to_operand_aliasing={{0}: (8, {}), {1}: (9, {}), {2}: (10, {})} | custom-call | flops 1000 | bytes 1000 | tf_op jit(solution)/shard_map/pallas_call | solution.py:240
  235.5 9.3 %collective-permute-done.27.refs_2_ = bf16[1,384,512]{2,1,0:T(8,128)(2,1)S(1)} collective-permute-done((bf16[1,384,512]{2,1,0:T(8,128)(2,1)S(1)}, bf16[1,384,512]{2,1,0:T(8,128)(2,1)S(1)}, u32[]{:S(2)}, u32[]{:S(2)}) %collective-permute-start.27) | collective-permute-done | bytes 393248 | tf_op jit(solution)/shard_map/ppermute | solution.py:25
  248.4 5.7 %shard_map.127 = (bf16[2,384,256]{2,1,0:T(8,128)(2,1)}, f32[2,384,256]{2,1,0:T(8,128)}) custom-call(s32[2]{0:T(128)} %pad_add_fusion.own_ref, bf16[4,384,640]{2,1,0:T(8,128)(2,1)} %add_convert_fusion.refs_0_, bf16[4,384,512]{2,1,0:T(8,128)(2,1)} %add_convert_fusion.2.refs_1_, bf16[4,384,512]{2,1,0:T(8,128)(2,1)} %add_convert_fusion.1.refs_2_, ...), custom_call_target="tpu_custom_call" | custom-call | flops 1000 | bytes 1000 | tf_op jit(solution)/shard_map/pallas_call | solution.py:174
  254.1 5.4 %shard_map.128 = (bf16[384,3072]{1,0:T(8,128)(2,1)}, bf16[384,3072]{1,0:T(8,128)(2,1)}, bf16[384,3072]{1,0:T(8,128)(2,1)}) custom-call(f32[2,384,512]{2,1,0:T(8,128)} %get-tuple-element.144.refs_0_, bf16[2,384,512]{2,1,0:T(8,128)(2,1)} %copy-done.12, bf16[1,384,512]{2,1,0:T(8,128)(2,1)} %copy-done.26, ...), custom_call_target="tpu_custom_call", output_to_operand_aliasing={{0}: (8, {}), {1}: (9, {}), {2}: (10, {})} | custom-call | flops 1000 | bytes 1000 | tf_op jit(solution)/shard_map/pallas_call | solution.py:240
  259.5 10.0 %collective-permute-done.29.refs_2_ = bf16[1,384,512]{2,1,0:T(8,128)(2,1)S(1)} collective-permute-done((bf16[1,384,512]{2,1,0:T(8,128)(2,1)S(1)}, bf16[1,384,512]{2,1,0:T(8,128)(2,1)S(1)}, u32[]{:S(2)}, u32[]{:S(2)}) %collective-permute-start.29) | collective-permute-done | bytes 393248 | tf_op jit(solution)/shard_map/ppermute | solution.py:25
  275.1 5.3 %shard_map.129 = (bf16[384,3072]{1,0:T(8,128)(2,1)}, bf16[384,3072]{1,0:T(8,128)(2,1)}, bf16[384,3072]{1,0:T(8,128)(2,1)}) custom-call(f32[2,384,512]{2,1,0:T(8,128)} %get-tuple-element.150.refs_0_, bf16[2,384,512]{2,1,0:T(8,128)(2,1)} %copy-done.10, bf16[1,384,512]{2,1,0:T(8,128)(2,1)} %copy-done.25, ...), custom_call_target="tpu_custom_call", output_to_operand_aliasing={{0}: (8, {}), {1}: (9, {}), {2}: (10, {})} | custom-call | flops 1000 | bytes 1000 | tf_op jit(solution)/shard_map/pallas_call | solution.py:240
  280.4 10.3 %collective-permute-done.31.refs_2_ = bf16[1,384,512]{2,1,0:T(8,128)(2,1)S(1)} collective-permute-done((bf16[1,384,512]{2,1,0:T(8,128)(2,1)S(1)}, bf16[1,384,512]{2,1,0:T(8,128)(2,1)S(1)}, u32[]{:S(2)}, u32[]{:S(2)}) %collective-permute-start.31) | collective-permute-done | bytes 393248 | tf_op jit(solution)/shard_map/ppermute | solution.py:25
  295.5 5.3 %shard_map.130 = (bf16[384,3072]{1,0:T(8,128)(2,1)}, bf16[384,3072]{1,0:T(8,128)(2,1)}, bf16[384,3072]{1,0:T(8,128)(2,1)}) custom-call(f32[2,384,512]{2,1,0:T(8,128)} %get-tuple-element.156.refs_0_, bf16[2,384,512]{2,1,0:T(8,128)(2,1)} %copy-done.11, bf16[1,384,512]{2,1,0:T(8,128)(2,1)} %copy-done.27, ...), custom_call_target="tpu_custom_call", output_to_operand_aliasing={{0}: (8, {}), {1}: (9, {}), {2}: (10, {})} | custom-call | flops 1000 | bytes 1000 | tf_op jit(solution)/shard_map/pallas_call | solution.py:240
  309.4 5.6 %collective-permute-done.35.refs_2_ = bf16[1,384,256]{2,1,0:T(8,128)(2,1)S(1)} collective-permute-done((bf16[1,384,256]{2,1,0:T(8,128)(2,1)S(1)}, bf16[1,384,256]{2,1,0:T(8,128)(2,1)S(1)}, u32[]{:S(2)}, u32[]{:S(2)}) %collective-permute-start.35) | collective-permute-done | bytes 196640 | tf_op jit(solution)/shard_map/ppermute | solution.py:25
  (178 shorter events, 120.2 us)
Async XLA Ops:
  7.2 131.9 %all-gather.5.cloned.1.call-start = ((), (), s32[]{:S(2)}) async-start(), calls=%async_computation.1 | async-start | bytes 6389760 | tf_op jit(solution)/shard_map/all_gather | solution.py:324
  10.8 179.8 %all-gather.3.cloned.1.call-start = ((), (), s32[]{:S(2)}) async-start(), calls=%async_computation | async-start | bytes 6389760 | tf_op jit(solution)/shard_map/all_gather | solution.py:324
  36.0 40.5 %collective-permute-start.6 = (bf16[2,192,640]{2,1,0:T(8,128)(2,1)}, bf16[2,192,640]{2,1,0:T(8,128)(2,1)S(1)}, u32[]{:S(2)}, u32[]{:S(2)}) collective-permute-start(bf16[2,192,640]{2,1,0:T(8,128)(2,1)} %get-tuple-element.91), channel_id=1, source_target_pairs={{0,2},{1,3},{2,0},{3,1},{4,6},{5,7},{6,4},{7,5},{8,10},{9,11},{10,... | collective-permute-start | bytes 1474568 | tf_op jit(solution)/shard_map/ppermute | solution.py:25
  36.4 41.7 %collective-permute-start.7 = (bf16[2,192,640]{2,1,0:T(8,128)(2,1)}, bf16[2,192,640]{2,1,0:T(8,128)(2,1)S(1)}, u32[]{:S(2)}, u32[]{:S(2)}) collective-permute-start(bf16[2,192,640]{2,1,0:T(8,128)(2,1)} %get-tuple-element.92), channel_id=1, source_target_pairs={{0,4},{1,5},{2,6},{3,7},{4,0},{5,1},{6,2},{7,3},{8,12},{9,13},{10,... | collective-permute-start | bytes 1474568 | tf_op jit(solution)/shard_map/ppermute | solution.py:25
  38.0 40.8 %collective-permute-start.8 = (bf16[2,192,640]{2,1,0:T(8,128)(2,1)}, bf16[2,192,640]{2,1,0:T(8,128)(2,1)S(1)}, u32[]{:S(2)}, u32[]{:S(2)}) collective-permute-start(bf16[2,192,640]{2,1,0:T(8,128)(2,1)} %get-tuple-element.93), channel_id=1, source_target_pairs={{0,6},{1,7},{2,4},{3,5},{4,2},{5,3},{6,0},{7,1},{8,14},{9,15},{10,... | collective-permute-start | bytes 1474568 | tf_op jit(solution)/shard_map/ppermute | solution.py:25
  42.8 29.4 %collective-permute-start.12 = (bf16[2,192,512]{2,1,0:T(8,128)(2,1)}, bf16[2,192,512]{2,1,0:T(8,128)(2,1)S(1)}, u32[]{:S(2)}, u32[]{:S(2)}) collective-permute-start(bf16[2,192,512]{2,1,0:T(8,128)(2,1)} %get-tuple-element.99), channel_id=1, source_target_pairs={{0,2},{1,3},{2,0},{3,1},{4,6},{5,7},{6,4},{7,5},{8,10},{9,11},{10,... | collective-permute-start | bytes 1179656 | tf_op jit(solution)/shard_map/ppermute | solution.py:25
  49.7 35.8 %collective-permute-start.13 = (bf16[2,192,512]{2,1,0:T(8,128)(2,1)}, bf16[2,192,512]{2,1,0:T(8,128)(2,1)S(1)}, u32[]{:S(2)}, u32[]{:S(2)}) collective-permute-start(bf16[2,192,512]{2,1,0:T(8,128)(2,1)} %get-tuple-element.100), channel_id=1, source_target_pairs={{0,4},{1,5},{2,6},{3,7},{4,0},{5,1},{6,2},{7,3},{8,12},{9,13},{10,... | collective-permute-start | bytes 1179656 | tf_op jit(solution)/shard_map/ppermute | solution.py:25
  72.2 21.5 %collective-permute-start.14 = (bf16[2,192,512]{2,1,0:T(8,128)(2,1)}, bf16[2,192,512]{2,1,0:T(8,128)(2,1)S(1)}, u32[]{:S(2)}, u32[]{:S(2)}) collective-permute-start(bf16[2,192,512]{2,1,0:T(8,128)(2,1)} %get-tuple-element.101), channel_id=1, source_target_pairs={{0,6},{1,7},{2,4},{3,5},{4,2},{5,3},{6,0},{7,1},{8,14},{9,15},{10,... | collective-permute-start | bytes 1179656 | tf_op jit(solution)/shard_map/ppermute | solution.py:25
  76.4 28.7 %collective-permute-start.18 = (bf16[2,192,512]{2,1,0:T(8,128)(2,1)}, bf16[2,192,512]{2,1,0:T(8,128)(2,1)}, u32[]{:S(2)}, u32[]{:S(2)}) collective-permute-start(bf16[2,192,512]{2,1,0:T(8,128)(2,1)} %get-tuple-element.107), channel_id=1, source_target_pairs={{0,2},{1,3},{2,0},{3,1},{4,6},{5,7},{6,4},{7,5},{8,10},{9,11},{10,... | collective-permute-start | bytes 1179656 | tf_op jit(solution)/shard_map/ppermute | solution.py:25
  78.1 27.1 %collective-permute-start.19 = (bf16[2,192,512]{2,1,0:T(8,128)(2,1)}, bf16[2,192,512]{2,1,0:T(8,128)(2,1)}, u32[]{:S(2)}, u32[]{:S(2)}) collective-permute-start(bf16[2,192,512]{2,1,0:T(8,128)(2,1)} %get-tuple-element.108), channel_id=1, source_target_pairs={{0,4},{1,5},{2,6},{3,7},{4,0},{5,1},{6,2},{7,3},{8,12},{9,13},{10,... | collective-permute-start | bytes 1179656 | tf_op jit(solution)/shard_map/ppermute | solution.py:25
  78.7 33.0 %collective-permute-start.20 = (bf16[2,192,512]{2,1,0:T(8,128)(2,1)}, bf16[2,192,512]{2,1,0:T(8,128)(2,1)}, u32[]{:S(2)}, u32[]{:S(2)}) collective-permute-start(bf16[2,192,512]{2,1,0:T(8,128)(2,1)} %get-tuple-element.109), channel_id=1, source_target_pairs={{0,6},{1,7},{2,4},{3,5},{4,2},{5,3},{6,0},{7,1},{8,14},{9,15},{10,... | collective-permute-start | bytes 1179656 | tf_op jit(solution)/shard_map/ppermute | solution.py:25
  116.1 15.9 %collective-permute-start.21 = (bf16[4,384,512]{2,1,0:T(8,128)(2,1)}, bf16[4,384,512]{2,1,0:T(8,128)(2,1)S(1)}, u32[]{:S(2)}, u32[]{:S(2)}) collective-permute-start(bf16[4,384,512]{2,1,0:T(8,128)(2,1)} %shard_map.118), channel_id=1, source_target_pairs={{0,1},{1,0},{2,3},{3,2},{4,5},{5,4},{6,7},{7,6},{8,9},{9,8},{10,11... | collective-permute-start | bytes 4718600 | tf_op jit(solution)/shard_map/ppermute | solution.py:25
  146.8 22.6 %collective-permute-start.22 = (bf16[2,384,512]{2,1,0:T(8,128)(2,1)}, bf16[2,384,512]{2,1,0:T(8,128)(2,1)S(1)}, u32[]{:S(2)}, u32[]{:S(2)}) collective-permute-start(bf16[2,384,512]{2,1,0:T(8,128)(2,1)} %get-tuple-element.113), channel_id=1, source_target_pairs={{0,8},{1,9},{2,10},{3,11},{4,12},{5,13},{6,14},{7,15},{8,0},{9,1},... | collective-permute-start | bytes 2359304 | tf_op jit(solution)/shard_map/ppermute | solution.py:25
  158.2 39.7 %collective-permute-start.24 = (bf16[2,384,512]{2,1,0:T(8,128)(2,1)}, bf16[2,384,512]{2,1,0:T(8,128)(2,1)}, u32[]{:S(2)}, u32[]{:S(2)}) collective-permute-start(bf16[2,384,512]{2,1,0:T(8,128)(2,1)} %get-tuple-element.115), channel_id=1, source_target_pairs={{0,8},{1,9},{2,10},{3,11},{4,12},{5,13},{6,14},{7,15},{8,0},{9,1},... | collective-permute-start | bytes 2359304 | tf_op jit(solution)/shard_map/ppermute | solution.py:25
  170.3 27.6 %collective-permute-start.23 = (bf16[1,384,512]{2,1,0:T(8,128)(2,1)S(1)}, bf16[1,384,512]{2,1,0:T(8,128)(2,1)S(1)}, u32[]{:S(2)}, u32[]{:S(2)}) collective-permute-start(bf16[1,384,512]{2,1,0:T(8,128)(2,1)S(1)} %add_convert_fusion.7), channel_id=1, source_target_pairs={{0,16},{1,17},{2,18},{3,19},{4,20},{5,21},{6,22},{7,23},{8,24},{9,... | collective-permute-start | bytes 1179656 | tf_op jit(solution)/shard_map/ppermute | solution.py:25
  174.3 45.6 %collective-permute-start.26 = (bf16[2,384,512]{2,1,0:T(8,128)(2,1)}, bf16[2,384,512]{2,1,0:T(8,128)(2,1)S(1)}, u32[]{:S(2)}, u32[]{:S(2)}) collective-permute-start(bf16[2,384,512]{2,1,0:T(8,128)(2,1)} %get-tuple-element.130), channel_id=1, source_target_pairs={{0,8},{1,9},{2,10},{3,11},{4,12},{5,13},{6,14},{7,15},{8,0},{9,1},... | collective-permute-start | bytes 2359304 | tf_op jit(solution)/shard_map/ppermute | solution.py:25
  199.2 20.2 %collective-permute-start.25 = (bf16[1,384,512]{2,1,0:T(8,128)(2,1)S(1)}, bf16[1,384,512]{2,1,0:T(8,128)(2,1)}, u32[]{:S(2)}, u32[]{:S(2)}) collective-permute-start(bf16[1,384,512]{2,1,0:T(8,128)(2,1)S(1)} %add_convert_fusion.6), channel_id=1, source_target_pairs={{0,16},{1,17},{2,18},{3,19},{4,20},{5,21},{6,22},{7,23},{8,24},{9,... | collective-permute-start | bytes 1179656 | tf_op jit(solution)/shard_map/ppermute | solution.py:25
  201.6 43.6 %collective-permute-start.28 = (bf16[2,384,512]{2,1,0:T(8,128)(2,1)}, bf16[2,384,512]{2,1,0:T(8,128)(2,1)S(1)}, u32[]{:S(2)}, u32[]{:S(2)}) collective-permute-start(bf16[2,384,512]{2,1,0:T(8,128)(2,1)} %get-tuple-element.138), channel_id=1, source_target_pairs={{0,8},{1,9},{2,10},{3,11},{4,12},{5,13},{6,14},{7,15},{8,0},{9,1},... | collective-permute-start | bytes 2359304 | tf_op jit(solution)/shard_map/ppermute | solution.py:25
  220.1 24.7 %collective-permute-start.27 = (bf16[1,384,512]{2,1,0:T(8,128)(2,1)S(1)}, bf16[1,384,512]{2,1,0:T(8,128)(2,1)S(1)}, u32[]{:S(2)}, u32[]{:S(2)}) collective-permute-start(bf16[1,384,512]{2,1,0:T(8,128)(2,1)S(1)} %add_convert_fusion.5), channel_id=1, source_target_pairs={{0,16},{1,17},{2,18},{3,19},{4,20},{5,21},{6,22},{7,23},{8,24},{9,... | collective-permute-start | bytes 1179656 | tf_op jit(solution)/shard_map/ppermute | solution.py:25
  223.2 47.0 %collective-permute-start.30 = (bf16[2,384,512]{2,1,0:T(8,128)(2,1)}, bf16[2,384,512]{2,1,0:T(8,128)(2,1)S(1)}, u32[]{:S(2)}, u32[]{:S(2)}) collective-permute-start(bf16[2,384,512]{2,1,0:T(8,128)(2,1)} %get-tuple-element.149), channel_id=1, source_target_pairs={{0,8},{1,9},{2,10},{3,11},{4,12},{5,13},{6,14},{7,15},{8,0},{9,1},... | collective-permute-start | bytes 2359304 | tf_op jit(solution)/shard_map/ppermute | solution.py:25
  245.4 24.1 %collective-permute-start.29 = (bf16[1,384,512]{2,1,0:T(8,128)(2,1)S(1)}, bf16[1,384,512]{2,1,0:T(8,128)(2,1)S(1)}, u32[]{:S(2)}, u32[]{:S(2)}) collective-permute-start(bf16[1,384,512]{2,1,0:T(8,128)(2,1)S(1)} %add_convert_fusion.4), channel_id=1, source_target_pairs={{0,16},{1,17},{2,18},{3,19},{4,20},{5,21},{6,22},{7,23},{8,24},{9,... | collective-permute-start | bytes 1179656 | tf_op jit(solution)/shard_map/ppermute | solution.py:25
  270.4 20.3 %collective-permute-start.31 = (bf16[1,384,512]{2,1,0:T(8,128)(2,1)S(1)}, bf16[1,384,512]{2,1,0:T(8,128)(2,1)S(1)}, u32[]{:S(2)}, u32[]{:S(2)}) collective-permute-start(bf16[1,384,512]{2,1,0:T(8,128)(2,1)S(1)} %add_convert_fusion.3), channel_id=1, source_target_pairs={{0,16},{1,17},{2,18},{3,19},{4,20},{5,21},{6,22},{7,23},{8,24},{9,... | collective-permute-start | bytes 1179656 | tf_op jit(solution)/shard_map/ppermute | solution.py:25
  273.1 18.0 %collective-permute-start.32 = (bf16[2,384,256]{2,1,0:T(8,128)(2,1)S(1)}, bf16[2,384,256]{2,1,0:T(8,128)(2,1)S(1)}, u32[]{:S(2)}, u32[]{:S(2)}) collective-permute-start(bf16[2,384,256]{2,1,0:T(8,128)(2,1)S(1)} %copy-done.36), channel_id=1, source_target_pairs={{0,8},{1,9},{2,10},{3,11},{4,12},{5,13},{6,14},{7,15},{8,0},{9,1},... | collective-permute-start | bytes 1179656 | tf_op jit(solution)/shard_map/ppermute | solution.py:25
  274.3 28.9 %collective-permute-start.34 = (bf16[2,384,256]{2,1,0:T(8,128)(2,1)S(1)}, bf16[2,384,256]{2,1,0:T(8,128)(2,1)S(1)}, u32[]{:S(2)}, u32[]{:S(2)}) collective-permute-start(bf16[2,384,256]{2,1,0:T(8,128)(2,1)S(1)} %copy-done.37), channel_id=1, source_target_pairs={{0,8},{1,9},{2,10},{3,11},{4,12},{5,13},{6,14},{7,15},{8,0},{9,1},... | collective-permute-start | bytes 1179656 | tf_op jit(solution)/shard_map/ppermute | solution.py:25
  (52 other events, 596.1 us)
Sparse Core Ops, SparseCore 0:
  10.9 102.0 all-gather.4
  116.2 74.2 all-gather.2

commit v3 on v2

--- a/solution.py
+++ b/solution.py
@@ -303,7 +303,8 @@
         for r in range(span):
             at = ((plane % span) ^ r) * width + start
             part = lax.dynamic_slice(grad_blocks, (0, at), (tok_count, size))
-            part = after(part, near)
+            if start:
+                part = after(part, near)
             parts.append(to_plane(part, r))
         plane_rows.append(parts)
         start += size
@@ -313,8 +314,8 @@
     sixth = n_heads // 6
     heads = [sixth] * 5 + ([sixth // 2] * 2 if sixth % 2 == 0 else [sixth])
     firsts = [sum(heads[:n]) for n in range(len(heads))]
-    group_of = [0, 0, 0] + [1] * (len(heads) - 3)
-    group_first = [0, 3 * sixth, n_heads]
+    group_of = [0, 0, 1, 1] + [2] * (len(heads) - 4)
+    group_first = [0, 2 * sixth, 4 * sixth, n_heads]
 
     def gather_weight(g, hold):
         part = weight[:, group_first[g] * HS : group_first[g + 1] * HS]
@@ -325,16 +326,16 @@
 
     weights = [gather_weight(0, None)]
 
-    rows, last, packed = [], None, None
+    rows, last, before, packed = [], None, None, None
     for parts in plane_rows:
         if packed is not None:
-            parts = [after(parts[0], packed[0])] + parts[1:]
+            parts = [after(parts[0], packed[0], *([] if before is None else [before]))] + parts[1:]
         packed = pack(position, scale, parts, planes * room)
         pieces = [packed[0]] + [send(packed[k], move=lambda p, c: (p ^ k, c)) for k in range(1, INNER)]
         if last is not None:
             pieces[0] = after(pieces[0], last)
         summed = place(slots, [one.reshape(span, planes, room, one.shape[2]) for one in pieces], tok_count)
-        last = summed
+        before, last = last, summed
         step = 1
         while step < cores:
             other = send(summed, move=lambda p, c: (p, c ^ step))
@@ -343,6 +344,7 @@
         rows.append(summed)
 
     weights.append(gather_weight(1, last))
+    weights.append(gather_weight(2, last))
 
     count = len(heads)
     last = rows[-1]
@@ -374,17 +376,15 @@
         old = attend(parts, firsts[n], heads[n], doc_ids, query_rows, key_rows, value_rows, old)
         last = old[0]
 
-    for n in range(3):
+    for n in range(2):
         multiply(n)
-        if n < 2:
-            launch(n, 0, leaving[n])
+        launch(n, 0, leaving[n])
     for n in range(count):
         for level in range(1, levels):
             pass_on(n, level, *(arrived[n - 1][-1:] if n else []))
         if n + 2 < count:
-            launch(n + 2, 0, after(leaving[n + 2], last))
-        if n + 3 < count:
-            multiply(n + 3)
+            multiply(n + 2)
+            launch(n + 2, 0, leaving[n + 2])
         if n >= 1:
             finish(n - 1)
     finish(count - 1)

time: 327 us -> 314 us (0.960)
  starting transfers between devices: 67.7 us -> 52 us
  local copies, waits for them, and re-layouts: 8.69 us -> 13.8 us
    ppermute x36, starting transfers between devices: 67.7 us -> 51.7 us  [swap(): return lax.ppermute(array, AXES, pairs)]
    all_gather x2 -> x3, waiting for transfers between devices: 16.2 us -> 3.3 us  [gather_weight(): lax.all_gather(part, 'peer', axis=0, tiled=True, axis_index_groups=members)]
    ppermute x36, waiting for transfers between devices: 102 us -> 112 us  [swap(): return lax.ppermute(array, AXES, pairs)]
    unnamed x76 -> x86, local copies, waits for them, and re-layouts: 2.35 us -> 6.3 us
  transfers between devices with their start and end apart: 38 -> 39, of which waited for: 22 -> 26; matrix products, arithmetic and copies ran while one was open for 4% -> 5% of each run, Pallas kernels for 32% -> 33%
where the time goes in v3:
time: 314 us; the launch traced here: 313 us
  waiting for transfers between devices  115 us (37%)
  Pallas kernels  107 us (34%)
  starting transfers between devices  52 us (17%)
  between operations  14.1 us (4%)
  local copies, waits for them, and re-layouts  13.8 us (4%)
  other arithmetic  10.8 us (3%)
    ppermute x36, waiting for transfers between devices, swap(): return lax.ppermute(array, AXES, pairs)  112 us
    ppermute x36, starting transfers between devices, swap(): return lax.ppermute(array, AXES, pairs)  51.7 us
    pallas_call x7, Pallas kernels, product(): pl.pallas_call(functools.partial(product_kernel, len(rows), len(pieces)),...  48.9 us
    pallas_call x7, Pallas kernels, attend(): pl.pallas_call(functools.partial(attend_kernel, heads, len(parts)), grid=...  33.6 us
    pallas_call x3, Pallas kernels, place(): pl.pallas_call(place_kernel, grid=(groups,), in_specs=[pl.BlockSpec((1, 1...  13.4 us
    pallas_call x3, Pallas kernels, pack(): pl.pallas_call(functools.partial(pack_kernel, sources), out_shape=[jax.Sh...  9.34 us
    convert_element_type x3, other arithmetic, shards(): (summed.astype(jnp.float32) + other.astype(jnp.float32)).astype(jnp.bfloa...  6.54 us
    unnamed x86, local copies, waits for them, and re-layouts  6.3 us
  transfers between devices with their start and end apart: 39, of which 26 were waited for; matrix products, arithmetic and copies ran while one was open for 5% of the time, Pallas kernels for 33%

profile of v3, /device:TPU:0, one launch (start us, length us, event | category | flops | bytes accessed | tf_op | source)
XLA Modules:
  0.0 312.7 jit_solution(10799937268346557763)
XLA Ops:
  41.5 7.5 %collective-permute-done.11.refs_1_ = bf16[384,512]{1,0:T(8,128)(2,1)S(1)} collective-permute-done((bf16[384,512]{1,0:T(8,128)(2,1)S(1)}, bf16[384,512]{1,0:T(8,128)(2,1)S(1)}, u32[]{:S(2)}, u32[]{:S(2)}) %collective-permute-start.11) | collective-permute-done | bytes 393248 | tf_op jit(solution)/shard_map/ppermute | solution.py:25
  61.0 8.2 %collective-permute-done.8 = bf16[2,192,640]{2,1,0:T(8,128)(2,1)S(1)} collective-permute-done((bf16[2,192,640]{2,1,0:T(8,128)(2,1)}, bf16[2,192,640]{2,1,0:T(8,128)(2,1)S(1)}, u32[]{:S(2)}, u32[]{:S(2)}) %collective-permute-start.8) | collective-permute-done | bytes 491552 | tf_op jit(solution)/shard_map/ppermute | solution.py:25
  82.6 5.6 %collective-permute-done.13 = bf16[2,192,512]{2,1,0:T(8,128)(2,1)S(1)} collective-permute-done((bf16[2,192,512]{2,1,0:T(8,128)(2,1)}, bf16[2,192,512]{2,1,0:T(8,128)(2,1)S(1)}, u32[]{:S(2)}, u32[]{:S(2)}) %collective-permute-start.13) | collective-permute-done | bytes 393248 | tf_op jit(solution)/shard_map/ppermute | solution.py:25
  96.0 9.2 %collective-permute-done.20 = bf16[2,192,512]{2,1,0:T(8,128)(2,1)S(1)} collective-permute-done((bf16[2,192,512]{2,1,0:T(8,128)(2,1)}, bf16[2,192,512]{2,1,0:T(8,128)(2,1)S(1)}, u32[]{:S(2)}, u32[]{:S(2)}) %collective-permute-start.20) | collective-permute-done | bytes 393248 | tf_op jit(solution)/shard_map/ppermute | solution.py:25
  110.7 8.5 %collective-permute-start.15 = (bf16[4,384,512]{2,1,0:T(8,128)(2,1)S(1)}, bf16[4,384,512]{2,1,0:T(8,128)(2,1)}, u32[]{:S(2)}, u32[]{:S(2)}) collective-permute-start(bf16[4,384,512]{2,1,0:T(8,128)(2,1)S(1)} %copy-done.1), channel_id=1, source_target_pairs={{0,1},{1,0},{2,3},{3,2},{4,5},{5,4},{6,7},{7,6},{8,9},{9,8},{10,11... | collective-permute-start | bytes 4718600 | tf_op jit(solution)/shard_map/ppermute | solution.py:25
  130.4 7.4 %shard_map.119 = (bf16[2,384,512]{2,1,0:T(8,128)(2,1)}, f32[2,384,512]{2,1,0:T(8,128)}) custom-call(s32[2]{0:T(128)} %pad_add_fusion.own_ref, bf16[4,384,640]{2,1,0:T(8,128)(2,1)} %add_convert_fusion.refs_0_, bf16[4,384,512]{2,1,0:T(8,128)(2,1)} %add_convert_fusion.2.refs_1_, bf16[4,384,512]{2,1,0:T(8,128)(2,1)} %add_convert_fusion.1.refs_2_, ...), custom_call_target="tpu_custom_call" | custom-call | flops 1000 | bytes 1000 | tf_op jit(solution)/shard_map/pallas_call | solution.py:174
  138.9 7.7 %shard_map.120 = (bf16[2,384,512]{2,1,0:T(8,128)(2,1)}, f32[2,384,512]{2,1,0:T(8,128)}) custom-call(s32[2]{0:T(128)} %pad_add_fusion.own_ref, bf16[4,384,640]{2,1,0:T(8,128)(2,1)} %add_convert_fusion.refs_0_, bf16[4,384,512]{2,1,0:T(8,128)(2,1)} %add_convert_fusion.2.refs_1_, bf16[4,384,512]{2,1,0:T(8,128)(2,1)} %add_convert_fusion.1.refs_2_, ...), custom_call_target="tpu_custom_call" | custom-call | flops 1000 | bytes 1000 | tf_op jit(solution)/shard_map/pallas_call | solution.py:174
  147.6 10.8 %collective-permute-done.22.refs_1_ = bf16[2,384,512]{2,1,0:T(8,128)(2,1)S(1)} collective-permute-done((bf16[2,384,512]{2,1,0:T(8,128)(2,1)}, bf16[2,384,512]{2,1,0:T(8,128)(2,1)S(1)}, u32[]{:S(2)}, u32[]{:S(2)}) %collective-permute-start.22) | collective-permute-done | bytes 786464 | tf_op jit(solution)/shard_map/ppermute | solution.py:25
  163.4 7.4 %shard_map.121 = (bf16[2,384,512]{2,1,0:T(8,128)(2,1)}, f32[2,384,512]{2,1,0:T(8,128)}) custom-call(s32[2]{0:T(128)} %pad_add_fusion.own_ref, bf16[4,384,640]{2,1,0:T(8,128)(2,1)} %add_convert_fusion.refs_0_, bf16[4,384,512]{2,1,0:T(8,128)(2,1)} %add_convert_fusion.2.refs_1_, bf16[4,384,512]{2,1,0:T(8,128)(2,1)} %add_convert_fusion.1.refs_2_, ...), custom_call_target="tpu_custom_call" | custom-call | flops 1000 | bytes 1000 | tf_op jit(solution)/shard_map/pallas_call | solution.py:174
  172.4 9.9 %collective-permute-done.23.refs_2_ = bf16[1,384,512]{2,1,0:T(8,128)(2,1)S(1)} collective-permute-done((bf16[1,384,512]{2,1,0:T(8,128)(2,1)S(1)}, bf16[1,384,512]{2,1,0:T(8,128)(2,1)S(1)}, u32[]{:S(2)}, u32[]{:S(2)}) %collective-permute-start.23) | collective-permute-done | bytes 393248 | tf_op jit(solution)/shard_map/ppermute | solution.py:25
  185.9 7.5 %shard_map.122 = (bf16[2,384,512]{2,1,0:T(8,128)(2,1)}, f32[2,384,512]{2,1,0:T(8,128)}) custom-call(s32[2]{0:T(128)} %pad_add_fusion.own_ref, bf16[4,384,640]{2,1,0:T(8,128)(2,1)} %add_convert_fusion.refs_0_, bf16[4,384,512]{2,1,0:T(8,128)(2,1)} %add_convert_fusion.2.refs_1_, bf16[4,384,512]{2,1,0:T(8,128)(2,1)} %add_convert_fusion.1.refs_2_, ...), custom_call_target="tpu_custom_call" | custom-call | flops 1000 | bytes 1000 | tf_op jit(solution)/shard_map/pallas_call | solution.py:174
  194.3 5.3 %shard_map.123 = (bf16[384,3072]{1,0:T(8,128)(2,1)}, bf16[384,3072]{1,0:T(8,128)(2,1)}, bf16[384,3072]{1,0:T(8,128)(2,1)}) custom-call(f32[2,384,512]{2,1,0:T(8,128)} %get-tuple-element.117.refs_0_, bf16[2,384,512]{2,1,0:T(8,128)(2,1)} %copy-done.14, bf16[1,384,512]{2,1,0:T(8,128)(2,1)} %copy-done.35, s32[1,384]{1,0:T(1,128)} %refs_3_.13, ...), custom_call_target="tpu_custom_call" | custom-call | flops 1000 | bytes 1000 | tf_op jit(solution)/shard_map/pallas_call | solution.py:240
  199.6 7.9 %collective-permute-done.25.refs_2_ = bf16[1,384,512]{2,1,0:T(8,128)(2,1)S(1)} collective-permute-done((bf16[1,384,512]{2,1,0:T(8,128)(2,1)S(1)}, bf16[1,384,512]{2,1,0:T(8,128)(2,1)S(1)}, u32[]{:S(2)}, u32[]{:S(2)}) %collective-permute-start.25) | collective-permute-done | bytes 393248 | tf_op jit(solution)/shard_map/ppermute | solution.py:25
  212.3 7.4 %shard_map.124 = (bf16[2,384,512]{2,1,0:T(8,128)(2,1)}, f32[2,384,512]{2,1,0:T(8,128)}) custom-call(s32[2]{0:T(128)} %pad_add_fusion.own_ref, bf16[4,384,640]{2,1,0:T(8,128)(2,1)} %add_convert_fusion.refs_0_, bf16[4,384,512]{2,1,0:T(8,128)(2,1)} %add_convert_fusion.2.refs_1_, bf16[4,384,512]{2,1,0:T(8,128)(2,1)} %add_convert_fusion.1.refs_2_, ...), custom_call_target="tpu_custom_call" | custom-call | flops 1000 | bytes 1000 | tf_op jit(solution)/shard_map/pallas_call | solution.py:174
  220.4 5.3 %shard_map.125 = (bf16[384,3072]{1,0:T(8,128)(2,1)}, bf16[384,3072]{1,0:T(8,128)(2,1)}, bf16[384,3072]{1,0:T(8,128)(2,1)}) custom-call(f32[2,384,512]{2,1,0:T(8,128)} %get-tuple-element.124.refs_0_, bf16[2,384,512]{2,1,0:T(8,128)(2,1)} %copy-done.13, bf16[1,384,512]{2,1,0:T(8,128)(2,1)} %copy-done.32, ...), custom_call_target="tpu_custom_call", output_to_operand_aliasing={{0}: (8, {}), {1}: (9, {}), {2}: (10, {})} | custom-call | flops 1000 | bytes 1000 | tf_op jit(solution)/shard_map/pallas_call | solution.py:240
  225.8 7.1 %collective-permute-done.27.refs_2_ = bf16[1,384,512]{2,1,0:T(8,128)(2,1)S(1)} collective-permute-done((bf16[1,384,512]{2,1,0:T(8,128)(2,1)S(1)}, bf16[1,384,512]{2,1,0:T(8,128)(2,1)S(1)}, u32[]{:S(2)}, u32[]{:S(2)}) %collective-permute-start.27) | collective-permute-done | bytes 393248 | tf_op jit(solution)/shard_map/ppermute | solution.py:25
  236.4 5.7 %shard_map.126 = (bf16[2,384,256]{2,1,0:T(8,128)(2,1)}, f32[2,384,256]{2,1,0:T(8,128)}) custom-call(s32[2]{0:T(128)} %pad_add_fusion.own_ref, bf16[4,384,640]{2,1,0:T(8,128)(2,1)} %add_convert_fusion.refs_0_, bf16[4,384,512]{2,1,0:T(8,128)(2,1)} %add_convert_fusion.2.refs_1_, bf16[4,384,512]{2,1,0:T(8,128)(2,1)} %add_convert_fusion.1.refs_2_, ...), custom_call_target="tpu_custom_call" | custom-call | flops 1000 | bytes 1000 | tf_op jit(solution)/shard_map/pallas_call | solution.py:174
  242.2 5.4 %shard_map.127 = (bf16[384,3072]{1,0:T(8,128)(2,1)}, bf16[384,3072]{1,0:T(8,128)(2,1)}, bf16[384,3072]{1,0:T(8,128)(2,1)}) custom-call(f32[2,384,512]{2,1,0:T(8,128)} %get-tuple-element.131.refs_0_, bf16[2,384,512]{2,1,0:T(8,128)(2,1)} %collective-permute-done.26.refs_1_, ...), custom_call_target="tpu_custom_call", output_to_operand_aliasing={{0}: (8, {}), {1}: (9, {}), {2}: (10, {})} | custom-call | flops 1000 | bytes 1000 | tf_op jit(solution)/shard_map/pallas_call | solution.py:240
  247.5 10.0 %collective-permute-done.29.refs_2_ = bf16[1,384,512]{2,1,0:T(8,128)(2,1)S(1)} collective-permute-done((bf16[1,384,512]{2,1,0:T(8,128)(2,1)S(1)}, bf16[1,384,512]{2,1,0:T(8,128)(2,1)S(1)}, u32[]{:S(2)}, u32[]{:S(2)}) %collective-permute-start.29) | collective-permute-done | bytes 393248 | tf_op jit(solution)/shard_map/ppermute | solution.py:25
  261.1 5.8 %shard_map.128 = (bf16[2,384,256]{2,1,0:T(8,128)(2,1)}, f32[2,384,256]{2,1,0:T(8,128)}) custom-call(s32[2]{0:T(128)} %pad_add_fusion.own_ref, bf16[4,384,640]{2,1,0:T(8,128)(2,1)} %add_convert_fusion.refs_0_, bf16[4,384,512]{2,1,0:T(8,128)(2,1)} %add_convert_fusion.2.refs_1_, bf16[4,384,512]{2,1,0:T(8,128)(2,1)} %add_convert_fusion.1.refs_2_, ...), custom_call_target="tpu_custom_call" | custom-call | flops 1000 | bytes 1000 | tf_op jit(solution)/shard_map/pallas_call | solution.py:174
  269.0 5.3 %shard_map.129 = (bf16[384,3072]{1,0:T(8,128)(2,1)}, bf16[384,3072]{1,0:T(8,128)(2,1)}, bf16[384,3072]{1,0:T(8,128)(2,1)}) custom-call(f32[2,384,512]{2,1,0:T(8,128)} %get-tuple-element.140.refs_0_, bf16[2,384,512]{2,1,0:T(8,128)(2,1)} %copy-done.11, bf16[1,384,512]{2,1,0:T(8,128)(2,1)} %copy-done.31, ...), custom_call_target="tpu_custom_call", output_to_operand_aliasing={{0}: (8, {}), {1}: (9, {}), {2}: (10, {})} | custom-call | flops 1000 | bytes 1000 | tf_op jit(solution)/shard_map/pallas_call | solution.py:240
  274.3 4.7 %collective-permute-done.31.refs_2_ = bf16[1,384,512]{2,1,0:T(8,128)(2,1)S(1)} collective-permute-done((bf16[1,384,512]{2,1,0:T(8,128)(2,1)S(1)}, bf16[1,384,512]{2,1,0:T(8,128)(2,1)S(1)}, u32[]{:S(2)}, u32[]{:S(2)}) %collective-permute-start.31) | collective-permute-done | bytes 393248 | tf_op jit(solution)/shard_map/ppermute | solution.py:25
  281.7 5.3 %shard_map.130 = (bf16[384,3072]{1,0:T(8,128)(2,1)}, bf16[384,3072]{1,0:T(8,128)(2,1)}, bf16[384,3072]{1,0:T(8,128)(2,1)}) custom-call(f32[2,384,512]{2,1,0:T(8,128)} %get-tuple-element.145.refs_0_, bf16[2,384,512]{2,1,0:T(8,128)(2,1)} %copy-done.12, bf16[1,384,512]{2,1,0:T(8,128)(2,1)} %copy-done.33, ...), custom_call_target="tpu_custom_call", output_to_operand_aliasing={{0}: (8, {}), {1}: (9, {}), {2}: (10, {})} | custom-call | flops 1000 | bytes 1000 | tf_op jit(solution)/shard_map/pallas_call | solution.py:240
  287.0 5.3 %collective-permute-done.33.refs_2_ = bf16[1,384,256]{2,1,0:T(8,128)(2,1)S(1)} collective-permute-done((bf16[1,384,256]{2,1,0:T(8,128)(2,1)S(1)}, bf16[1,384,256]{2,1,0:T(8,128)(2,1)S(1)}, u32[]{:S(2)}, u32[]{:S(2)}) %collective-permute-start.33) | collective-permute-done | bytes 196640 | tf_op jit(solution)/shard_map/ppermute | solution.py:25
  (191 shorter events, 128.5 us)
Async XLA Ops:
  7.2 123.3 %all-gather.8.cloned.1.call-start = ((), (), s32[]{:S(2)}) async-start(), calls=%async_computation.2 | async-start | bytes 4259840 | tf_op jit(solution)/shard_map/all_gather | solution.py:325
  10.6 152.8 %all-gather.6.cloned.1.call-start = ((), (), s32[]{:S(2)}) async-start(), calls=%async_computation.1 | async-start | bytes 4259840 | tf_op jit(solution)/shard_map/all_gather | solution.py:325
  34.7 18.0 %collective-permute-start.6 = (bf16[2,192,640]{2,1,0:T(8,128)(2,1)}, bf16[2,192,640]{2,1,0:T(8,128)(2,1)S(1)}, u32[]{:S(2)}, u32[]{:S(2)}) collective-permute-start(bf16[2,192,640]{2,1,0:T(8,128)(2,1)} %get-tuple-element.83), channel_id=1, source_target_pairs={{0,2},{1,3},{2,0},{3,1},{4,6},{5,7},{6,4},{7,5},{8,10},{9,11},{10,... | collective-permute-start | bytes 1474568 | tf_op jit(solution)/shard_map/ppermute | solution.py:25
  36.9 21.2 %collective-permute-start.7 = (bf16[2,192,640]{2,1,0:T(8,128)(2,1)}, bf16[2,192,640]{2,1,0:T(8,128)(2,1)S(1)}, u32[]{:S(2)}, u32[]{:S(2)}) collective-permute-start(bf16[2,192,640]{2,1,0:T(8,128)(2,1)} %get-tuple-element.84), channel_id=1, source_target_pairs={{0,4},{1,5},{2,6},{3,7},{4,0},{5,1},{6,2},{7,3},{8,12},{9,13},{10,... | collective-permute-start | bytes 1474568 | tf_op jit(solution)/shard_map/ppermute | solution.py:25
  38.4 30.8 %collective-permute-start.8 = (bf16[2,192,640]{2,1,0:T(8,128)(2,1)}, bf16[2,192,640]{2,1,0:T(8,128)(2,1)S(1)}, u32[]{:S(2)}, u32[]{:S(2)}) collective-permute-start(bf16[2,192,640]{2,1,0:T(8,128)(2,1)} %get-tuple-element.85), channel_id=1, source_target_pairs={{0,6},{1,7},{2,4},{3,5},{4,2},{5,3},{6,0},{7,1},{8,14},{9,15},{10,... | collective-permute-start | bytes 1474568 | tf_op jit(solution)/shard_map/ppermute | solution.py:25
  39.8 34.8 %collective-permute-start.16 = (bf16[384,512]{1,0:T(8,128)(2,1)}, bf16[384,512]{1,0:T(8,128)(2,1)S(1)}, u32[]{:S(2)}, u32[]{:S(2)}) collective-permute-start(bf16[384,512]{1,0:T(8,128)(2,1)} %get-tuple-element.94), channel_id=1, source_target_pairs={{0,0},{1,16},{2,2},{3,18},{4,4},{5,20},{6,6},{7,22},{8,8},{9,24},{... | collective-permute-start | bytes 1179656 | tf_op jit(solution)/shard_map/ppermute | solution.py:25
  48.9 25.7 %collective-permute-start.17 = (bf16[384,512]{1,0:T(8,128)(2,1)}, bf16[384,512]{1,0:T(8,128)(2,1)S(1)}, u32[]{:S(2)}, u32[]{:S(2)}) collective-permute-start(bf16[384,512]{1,0:T(8,128)(2,1)} %get-tuple-element.96), channel_id=1, source_target_pairs={{0,8},{1,24},{2,10},{3,26},{4,12},{5,28},{6,14},{7,30},{8,0},{9,16... | collective-permute-start | bytes 1179656 | tf_op jit(solution)/shard_map/ppermute | solution.py:25
  52.7 29.1 %collective-permute-start.12 = (bf16[2,192,512]{2,1,0:T(8,128)(2,1)}, bf16[2,192,512]{2,1,0:T(8,128)(2,1)S(1)}, u32[]{:S(2)}, u32[]{:S(2)}) collective-permute-start(bf16[2,192,512]{2,1,0:T(8,128)(2,1)} %get-tuple-element.91), channel_id=1, source_target_pairs={{0,2},{1,3},{2,0},{3,1},{4,6},{5,7},{6,4},{7,5},{8,10},{9,11},{10,... | collective-permute-start | bytes 1179656 | tf_op jit(solution)/shard_map/ppermute | solution.py:25
  58.1 30.1 %collective-permute-start.13 = (bf16[2,192,512]{2,1,0:T(8,128)(2,1)}, bf16[2,192,512]{2,1,0:T(8,128)(2,1)S(1)}, u32[]{:S(2)}, u32[]{:S(2)}) collective-permute-start(bf16[2,192,512]{2,1,0:T(8,128)(2,1)} %get-tuple-element.92), channel_id=1, source_target_pairs={{0,4},{1,5},{2,6},{3,7},{4,0},{5,1},{6,2},{7,3},{8,12},{9,13},{10,... | collective-permute-start | bytes 1179656 | tf_op jit(solution)/shard_map/ppermute | solution.py:25
  69.2 19.4 %collective-permute-start.14 = (bf16[2,192,512]{2,1,0:T(8,128)(2,1)}, bf16[2,192,512]{2,1,0:T(8,128)(2,1)S(1)}, u32[]{:S(2)}, u32[]{:S(2)}) collective-permute-start(bf16[2,192,512]{2,1,0:T(8,128)(2,1)} %get-tuple-element.93), channel_id=1, source_target_pairs={{0,6},{1,7},{2,4},{3,5},{4,2},{5,3},{6,0},{7,1},{8,14},{9,15},{10,... | collective-permute-start | bytes 1179656 | tf_op jit(solution)/shard_map/ppermute | solution.py:25
  81.8 23.4 %collective-permute-start.20 = (bf16[2,192,512]{2,1,0:T(8,128)(2,1)}, bf16[2,192,512]{2,1,0:T(8,128)(2,1)S(1)}, u32[]{:S(2)}, u32[]{:S(2)}) collective-permute-start(bf16[2,192,512]{2,1,0:T(8,128)(2,1)} %get-tuple-element.101), channel_id=1, source_target_pairs={{0,6},{1,7},{2,4},{3,5},{4,2},{5,3},{6,0},{7,1},{8,14},{9,15},{10,... | collective-permute-start | bytes 1179656 | tf_op jit(solution)/shard_map/ppermute | solution.py:25
  110.4 101.8 %all-gather.4.cloned.1.call-start = ((), (), s32[]{:S(2)}) async-start(), calls=%async_computation | async-start | bytes 4259840 | tf_op jit(solution)/shard_map/all_gather | solution.py:325
  137.8 20.6 %collective-permute-start.22 = (bf16[2,384,512]{2,1,0:T(8,128)(2,1)}, bf16[2,384,512]{2,1,0:T(8,128)(2,1)S(1)}, u32[]{:S(2)}, u32[]{:S(2)}) collective-permute-start(bf16[2,384,512]{2,1,0:T(8,128)(2,1)} %get-tuple-element.106), channel_id=1, source_target_pairs={{0,8},{1,9},{2,10},{3,11},{4,12},{5,13},{6,14},{7,15},{8,0},{9,1},... | collective-permute-start | bytes 2359304 | tf_op jit(solution)/shard_map/ppermute | solution.py:25
  146.6 37.1 %collective-permute-start.24 = (bf16[2,384,512]{2,1,0:T(8,128)(2,1)}, bf16[2,384,512]{2,1,0:T(8,128)(2,1)S(1)}, u32[]{:S(2)}, u32[]{:S(2)}) collective-permute-start(bf16[2,384,512]{2,1,0:T(8,128)(2,1)} %get-tuple-element.108), channel_id=1, source_target_pairs={{0,8},{1,9},{2,10},{3,11},{4,12},{5,13},{6,14},{7,15},{8,0},{9,1},... | collective-permute-start | bytes 2359304 | tf_op jit(solution)/shard_map/ppermute | solution.py:25
  159.3 23.0 %collective-permute-start.23 = (bf16[1,384,512]{2,1,0:T(8,128)(2,1)S(1)}, bf16[1,384,512]{2,1,0:T(8,128)(2,1)S(1)}, u32[]{:S(2)}, u32[]{:S(2)}) collective-permute-start(bf16[1,384,512]{2,1,0:T(8,128)(2,1)S(1)} %add_convert_fusion.7), channel_id=1, source_target_pairs={{0,16},{1,17},{2,18},{3,19},{4,20},{5,21},{6,22},{7,23},{8,24},{9,... | collective-permute-start | bytes 1179656 | tf_op jit(solution)/shard_map/ppermute | solution.py:25
  170.9 38.2 %collective-permute-start.26 = (bf16[2,384,512]{2,1,0:T(8,128)(2,1)}, bf16[2,384,512]{2,1,0:T(8,128)(2,1)}, u32[]{:S(2)}, u32[]{:S(2)}) collective-permute-start(bf16[2,384,512]{2,1,0:T(8,128)(2,1)} %get-tuple-element.113), channel_id=1, source_target_pairs={{0,8},{1,9},{2,10},{3,11},{4,12},{5,13},{6,14},{7,15},{8,0},{9,1},... | collective-permute-start | bytes 2359304 | tf_op jit(solution)/shard_map/ppermute | solution.py:25
  183.8 23.7 %collective-permute-start.25 = (bf16[1,384,512]{2,1,0:T(8,128)(2,1)S(1)}, bf16[1,384,512]{2,1,0:T(8,128)(2,1)S(1)}, u32[]{:S(2)}, u32[]{:S(2)}) collective-permute-start(bf16[1,384,512]{2,1,0:T(8,128)(2,1)S(1)} %add_convert_fusion.6), channel_id=1, source_target_pairs={{0,16},{1,17},{2,18},{3,19},{4,20},{5,21},{6,22},{7,23},{8,24},{9,... | collective-permute-start | bytes 1179656 | tf_op jit(solution)/shard_map/ppermute | solution.py:25
  193.4 40.9 %collective-permute-start.28 = (bf16[2,384,512]{2,1,0:T(8,128)(2,1)}, bf16[2,384,512]{2,1,0:T(8,128)(2,1)S(1)}, u32[]{:S(2)}, u32[]{:S(2)}) collective-permute-start(bf16[2,384,512]{2,1,0:T(8,128)(2,1)} %get-tuple-element.116), channel_id=1, source_target_pairs={{0,8},{1,9},{2,10},{3,11},{4,12},{5,13},{6,14},{7,15},{8,0},{9,1},... | collective-permute-start | bytes 2359304 | tf_op jit(solution)/shard_map/ppermute | solution.py:25
  210.2 22.6 %collective-permute-start.27 = (bf16[1,384,512]{2,1,0:T(8,128)(2,1)S(1)}, bf16[1,384,512]{2,1,0:T(8,128)(2,1)S(1)}, u32[]{:S(2)}, u32[]{:S(2)}) collective-permute-start(bf16[1,384,512]{2,1,0:T(8,128)(2,1)S(1)} %add_convert_fusion.5), channel_id=1, source_target_pairs={{0,16},{1,17},{2,18},{3,19},{4,20},{5,21},{6,22},{7,23},{8,24},{9,... | collective-permute-start | bytes 1179656 | tf_op jit(solution)/shard_map/ppermute | solution.py:25
  219.7 39.3 %collective-permute-start.30 = (bf16[2,384,512]{2,1,0:T(8,128)(2,1)}, bf16[2,384,512]{2,1,0:T(8,128)(2,1)S(1)}, u32[]{:S(2)}, u32[]{:S(2)}) collective-permute-start(bf16[2,384,512]{2,1,0:T(8,128)(2,1)} %get-tuple-element.123), channel_id=1, source_target_pairs={{0,8},{1,9},{2,10},{3,11},{4,12},{5,13},{6,14},{7,15},{8,0},{9,1},... | collective-permute-start | bytes 2359304 | tf_op jit(solution)/shard_map/ppermute | solution.py:25
  234.4 23.2 %collective-permute-start.29 = (bf16[1,384,512]{2,1,0:T(8,128)(2,1)S(1)}, bf16[1,384,512]{2,1,0:T(8,128)(2,1)S(1)}, u32[]{:S(2)}, u32[]{:S(2)}) collective-permute-start(bf16[1,384,512]{2,1,0:T(8,128)(2,1)S(1)} %add_convert_fusion.4), channel_id=1, source_target_pairs={{0,16},{1,17},{2,18},{3,19},{4,20},{5,21},{6,22},{7,23},{8,24},{9,... | collective-permute-start | bytes 1179656 | tf_op jit(solution)/shard_map/ppermute | solution.py:25
  259.1 19.9 %collective-permute-start.31 = (bf16[1,384,512]{2,1,0:T(8,128)(2,1)S(1)}, bf16[1,384,512]{2,1,0:T(8,128)(2,1)S(1)}, u32[]{:S(2)}, u32[]{:S(2)}) collective-permute-start(bf16[1,384,512]{2,1,0:T(8,128)(2,1)S(1)} %add_convert_fusion.3), channel_id=1, source_target_pairs={{0,16},{1,17},{2,18},{3,19},{4,20},{5,21},{6,22},{7,23},{8,24},{9,... | collective-permute-start | bytes 1179656 | tf_op jit(solution)/shard_map/ppermute | solution.py:25
  261.1 20.4 %collective-permute-start.32 = (bf16[2,384,256]{2,1,0:T(8,128)(2,1)S(1)}, bf16[2,384,256]{2,1,0:T(8,128)(2,1)S(1)}, u32[]{:S(2)}, u32[]{:S(2)}) collective-permute-start(bf16[2,384,256]{2,1,0:T(8,128)(2,1)S(1)} %copy-done.42), channel_id=1, source_target_pairs={{0,8},{1,9},{2,10},{3,11},{4,12},{5,13},{6,14},{7,15},{8,0},{9,1},... | collective-permute-start | bytes 1179656 | tf_op jit(solution)/shard_map/ppermute | solution.py:25
  266.9 25.5 %collective-permute-start.34 = (bf16[2,384,256]{2,1,0:T(8,128)(2,1)}, bf16[2,384,256]{2,1,0:T(8,128)(2,1)S(1)}, u32[]{:S(2)}, u32[]{:S(2)}) collective-permute-start(bf16[2,384,256]{2,1,0:T(8,128)(2,1)} %get-tuple-element.139), channel_id=1, source_target_pairs={{0,8},{1,9},{2,10},{3,11},{4,12},{5,13},{6,14},{7,15},{8,0},{9,1},... | collective-permute-start | bytes 1179656 | tf_op jit(solution)/shard_map/ppermute | solution.py:25
  (58 other events, 492.5 us)
Sparse Core Ops, SparseCore 0:
  10.7 68.0 all-gather.7
  110.5 52.8 all-gather.5
  165.3 46.2 all-gather.3

commit v4 on v3

--- a/solution.py
+++ b/solution.py
@@ -381,7 +381,7 @@
         launch(n, 0, leaving[n])
     for n in range(count):
         for level in range(1, levels):
-            pass_on(n, level, *(arrived[n - 1][-1:] if n else []))
+            pass_on(n, level, *(arrived[n - 1][-1:] if 0 < n < count - 1 else []))
         if n + 2 < count:
             multiply(n + 2)
             launch(n + 2, 0, leaving[n + 2])

time: 314 us -> 313 us (level)
  transfers between devices with their start and end apart: 39 -> 39, of which waited for: 26 -> 25; matrix products, arithmetic and copies ran while one was open for 5% -> 5% of each run, Pallas kernels for 33% -> 33%
where the time goes in v4:
time: 313 us; the launch traced here: 312 us
  waiting for transfers between devices  115 us (37%)
  Pallas kernels  107 us (34%)
  starting transfers between devices  50.6 us (16%)
  local copies, waits for them, and re-layouts  14.5 us (5%)
  between operations  14.1 us (5%)
  other arithmetic  10.8 us (3%)
    ppermute x36, waiting for transfers between devices, swap(): return lax.ppermute(array, AXES, pairs)  112 us
    ppermute x36, starting transfers between devices, swap(): return lax.ppermute(array, AXES, pairs)  50.3 us
    pallas_call x7, Pallas kernels, product(): pl.pallas_call(functools.partial(product_kernel, len(rows), len(pieces)),...  48.9 us
    pallas_call x7, Pallas kernels, attend(): pl.pallas_call(functools.partial(attend_kernel, heads, len(parts)), grid=...  33.6 us
    pallas_call x3, Pallas kernels, place(): pl.pallas_call(place_kernel, grid=(groups,), in_specs=[pl.BlockSpec((1, 1...  13.4 us
    pallas_call x3, Pallas kernels, pack(): pl.pallas_call(functools.partial(pack_kernel, sources), out_shape=[jax.Sh...  9.34 us
    unnamed x86, local copies, waits for them, and re-layouts  6.98 us
    convert_element_type x3, other arithmetic, shards(): (summed.astype(jnp.float32) + other.astype(jnp.float32)).astype(jnp.bfloa...  6.54 us
  transfers between devices with their start and end apart: 39, of which 25 were waited for; matrix products, arithmetic and copies ran while one was open for 5% of the time, Pallas kernels for 33%

profile of v4, /device:TPU:0, one launch (start us, length us, event | category | flops | bytes accessed | tf_op | source)
XLA Modules:
  0.0 312.1 jit_solution(7843560163113074905)
XLA Ops:
  41.5 7.5 %collective-permute-done.11.refs_1_ = bf16[384,512]{1,0:T(8,128)(2,1)S(1)} collective-permute-done((bf16[384,512]{1,0:T(8,128)(2,1)S(1)}, bf16[384,512]{1,0:T(8,128)(2,1)S(1)}, u32[]{:S(2)}, u32[]{:S(2)}) %collective-permute-start.11) | collective-permute-done | bytes 393248 | tf_op jit(solution)/shard_map/ppermute | solution.py:25
  61.0 8.2 %collective-permute-done.8 = bf16[2,192,640]{2,1,0:T(8,128)(2,1)S(1)} collective-permute-done((bf16[2,192,640]{2,1,0:T(8,128)(2,1)}, bf16[2,192,640]{2,1,0:T(8,128)(2,1)S(1)}, u32[]{:S(2)}, u32[]{:S(2)}) %collective-permute-start.8) | collective-permute-done | bytes 491552 | tf_op jit(solution)/shard_map/ppermute | solution.py:25
  82.6 5.6 %collective-permute-done.13 = bf16[2,192,512]{2,1,0:T(8,128)(2,1)S(1)} collective-permute-done((bf16[2,192,512]{2,1,0:T(8,128)(2,1)}, bf16[2,192,512]{2,1,0:T(8,128)(2,1)S(1)}, u32[]{:S(2)}, u32[]{:S(2)}) %collective-permute-start.13) | collective-permute-done | bytes 393248 | tf_op jit(solution)/shard_map/ppermute | solution.py:25
  96.0 9.2 %collective-permute-done.20 = bf16[2,192,512]{2,1,0:T(8,128)(2,1)S(1)} collective-permute-done((bf16[2,192,512]{2,1,0:T(8,128)(2,1)}, bf16[2,192,512]{2,1,0:T(8,128)(2,1)S(1)}, u32[]{:S(2)}, u32[]{:S(2)}) %collective-permute-start.20) | collective-permute-done | bytes 393248 | tf_op jit(solution)/shard_map/ppermute | solution.py:25
  110.7 8.5 %collective-permute-start.15 = (bf16[4,384,512]{2,1,0:T(8,128)(2,1)S(1)}, bf16[4,384,512]{2,1,0:T(8,128)(2,1)}, u32[]{:S(2)}, u32[]{:S(2)}) collective-permute-start(bf16[4,384,512]{2,1,0:T(8,128)(2,1)S(1)} %copy-done.1), channel_id=1, source_target_pairs={{0,1},{1,0},{2,3},{3,2},{4,5},{5,4},{6,7},{7,6},{8,9},{9,8},{10,11... | collective-permute-start | bytes 4718600 | tf_op jit(solution)/shard_map/ppermute | solution.py:25
  130.4 7.4 %shard_map.119 = (bf16[2,384,512]{2,1,0:T(8,128)(2,1)}, f32[2,384,512]{2,1,0:T(8,128)}) custom-call(s32[2]{0:T(128)} %pad_add_fusion.own_ref, bf16[4,384,640]{2,1,0:T(8,128)(2,1)} %add_convert_fusion.refs_0_, bf16[4,384,512]{2,1,0:T(8,128)(2,1)} %add_convert_fusion.2.refs_1_, bf16[4,384,512]{2,1,0:T(8,128)(2,1)} %add_convert_fusion.1.refs_2_, ...), custom_call_target="tpu_custom_call" | custom-call | flops 1000 | bytes 1000 | tf_op jit(solution)/shard_map/pallas_call | solution.py:174
  138.9 7.7 %shard_map.120 = (bf16[2,384,512]{2,1,0:T(8,128)(2,1)}, f32[2,384,512]{2,1,0:T(8,128)}) custom-call(s32[2]{0:T(128)} %pad_add_fusion.own_ref, bf16[4,384,640]{2,1,0:T(8,128)(2,1)} %add_convert_fusion.refs_0_, bf16[4,384,512]{2,1,0:T(8,128)(2,1)} %add_convert_fusion.2.refs_1_, bf16[4,384,512]{2,1,0:T(8,128)(2,1)} %add_convert_fusion.1.refs_2_, ...), custom_call_target="tpu_custom_call" | custom-call | flops 1000 | bytes 1000 | tf_op jit(solution)/shard_map/pallas_call | solution.py:174
  147.6 10.8 %collective-permute-done.22.refs_1_ = bf16[2,384,512]{2,1,0:T(8,128)(2,1)S(1)} collective-permute-done((bf16[2,384,512]{2,1,0:T(8,128)(2,1)}, bf16[2,384,512]{2,1,0:T(8,128)(2,1)S(1)}, u32[]{:S(2)}, u32[]{:S(2)}) %collective-permute-start.22) | collective-permute-done | bytes 786464 | tf_op jit(solution)/shard_map/ppermute | solution.py:25
  163.4 7.4 %shard_map.121 = (bf16[2,384,512]{2,1,0:T(8,128)(2,1)}, f32[2,384,512]{2,1,0:T(8,128)}) custom-call(s32[2]{0:T(128)} %pad_add_fusion.own_ref, bf16[4,384,640]{2,1,0:T(8,128)(2,1)} %add_convert_fusion.refs_0_, bf16[4,384,512]{2,1,0:T(8,128)(2,1)} %add_convert_fusion.2.refs_1_, bf16[4,384,512]{2,1,0:T(8,128)(2,1)} %add_convert_fusion.1.refs_2_, ...), custom_call_target="tpu_custom_call" | custom-call | flops 1000 | bytes 1000 | tf_op jit(solution)/shard_map/pallas_call | solution.py:174
  172.4 9.9 %collective-permute-done.23.refs_2_ = bf16[1,384,512]{2,1,0:T(8,128)(2,1)S(1)} collective-permute-done((bf16[1,384,512]{2,1,0:T(8,128)(2,1)S(1)}, bf16[1,384,512]{2,1,0:T(8,128)(2,1)S(1)}, u32[]{:S(2)}, u32[]{:S(2)}) %collective-permute-start.23) | collective-permute-done | bytes 393248 | tf_op jit(solution)/shard_map/ppermute | solution.py:25
  185.9 7.5 %shard_map.122 = (bf16[2,384,512]{2,1,0:T(8,128)(2,1)}, f32[2,384,512]{2,1,0:T(8,128)}) custom-call(s32[2]{0:T(128)} %pad_add_fusion.own_ref, bf16[4,384,640]{2,1,0:T(8,128)(2,1)} %add_convert_fusion.refs_0_, bf16[4,384,512]{2,1,0:T(8,128)(2,1)} %add_convert_fusion.2.refs_1_, bf16[4,384,512]{2,1,0:T(8,128)(2,1)} %add_convert_fusion.1.refs_2_, ...), custom_call_target="tpu_custom_call" | custom-call | flops 1000 | bytes 1000 | tf_op jit(solution)/shard_map/pallas_call | solution.py:174
  194.3 5.3 %shard_map.123 = (bf16[384,3072]{1,0:T(8,128)(2,1)}, bf16[384,3072]{1,0:T(8,128)(2,1)}, bf16[384,3072]{1,0:T(8,128)(2,1)}) custom-call(f32[2,384,512]{2,1,0:T(8,128)} %get-tuple-element.117.refs_0_, bf16[2,384,512]{2,1,0:T(8,128)(2,1)} %copy-done.14, bf16[1,384,512]{2,1,0:T(8,128)(2,1)} %copy-done.35, s32[1,384]{1,0:T(1,128)} %refs_3_.13, ...), custom_call_target="tpu_custom_call" | custom-call | flops 1000 | bytes 1000 | tf_op jit(solution)/shard_map/pallas_call | solution.py:240
  199.6 7.9 %collective-permute-done.25.refs_2_ = bf16[1,384,512]{2,1,0:T(8,128)(2,1)S(1)} collective-permute-done((bf16[1,384,512]{2,1,0:T(8,128)(2,1)S(1)}, bf16[1,384,512]{2,1,0:T(8,128)(2,1)S(1)}, u32[]{:S(2)}, u32[]{:S(2)}) %collective-permute-start.25) | collective-permute-done | bytes 393248 | tf_op jit(solution)/shard_map/ppermute | solution.py:25
  212.3 7.4 %shard_map.124 = (bf16[2,384,512]{2,1,0:T(8,128)(2,1)}, f32[2,384,512]{2,1,0:T(8,128)}) custom-call(s32[2]{0:T(128)} %pad_add_fusion.own_ref, bf16[4,384,640]{2,1,0:T(8,128)(2,1)} %add_convert_fusion.refs_0_, bf16[4,384,512]{2,1,0:T(8,128)(2,1)} %add_convert_fusion.2.refs_1_, bf16[4,384,512]{2,1,0:T(8,128)(2,1)} %add_convert_fusion.1.refs_2_, ...), custom_call_target="tpu_custom_call" | custom-call | flops 1000 | bytes 1000 | tf_op jit(solution)/shard_map/pallas_call | solution.py:174
  220.4 5.3 %shard_map.125 = (bf16[384,3072]{1,0:T(8,128)(2,1)}, bf16[384,3072]{1,0:T(8,128)(2,1)}, bf16[384,3072]{1,0:T(8,128)(2,1)}) custom-call(f32[2,384,512]{2,1,0:T(8,128)} %get-tuple-element.124.refs_0_, bf16[2,384,512]{2,1,0:T(8,128)(2,1)} %copy-done.13, bf16[1,384,512]{2,1,0:T(8,128)(2,1)} %copy-done.32, ...), custom_call_target="tpu_custom_call", output_to_operand_aliasing={{0}: (8, {}), {1}: (9, {}), {2}: (10, {})} | custom-call | flops 1000 | bytes 1000 | tf_op jit(solution)/shard_map/pallas_call | solution.py:240
  225.8 7.1 %collective-permute-done.27.refs_2_ = bf16[1,384,512]{2,1,0:T(8,128)(2,1)S(1)} collective-permute-done((bf16[1,384,512]{2,1,0:T(8,128)(2,1)S(1)}, bf16[1,384,512]{2,1,0:T(8,128)(2,1)S(1)}, u32[]{:S(2)}, u32[]{:S(2)}) %collective-permute-start.27) | collective-permute-done | bytes 393248 | tf_op jit(solution)/shard_map/ppermute | solution.py:25
  236.4 5.7 %shard_map.126 = (bf16[2,384,256]{2,1,0:T(8,128)(2,1)}, f32[2,384,256]{2,1,0:T(8,128)}) custom-call(s32[2]{0:T(128)} %pad_add_fusion.own_ref, bf16[4,384,640]{2,1,0:T(8,128)(2,1)} %add_convert_fusion.refs_0_, bf16[4,384,512]{2,1,0:T(8,128)(2,1)} %add_convert_fusion.2.refs_1_, bf16[4,384,512]{2,1,0:T(8,128)(2,1)} %add_convert_fusion.1.refs_2_, ...), custom_call_target="tpu_custom_call" | custom-call | flops 1000 | bytes 1000 | tf_op jit(solution)/shard_map/pallas_call | solution.py:174
  242.2 5.4 %shard_map.127 = (bf16[384,3072]{1,0:T(8,128)(2,1)}, bf16[384,3072]{1,0:T(8,128)(2,1)}, bf16[384,3072]{1,0:T(8,128)(2,1)}) custom-call(f32[2,384,512]{2,1,0:T(8,128)} %get-tuple-element.131.refs_0_, bf16[2,384,512]{2,1,0:T(8,128)(2,1)} %collective-permute-done.26.refs_1_, ...), custom_call_target="tpu_custom_call", output_to_operand_aliasing={{0}: (8, {}), {1}: (9, {}), {2}: (10, {})} | custom-call | flops 1000 | bytes 1000 | tf_op jit(solution)/shard_map/pallas_call | solution.py:240
  247.5 10.0 %collective-permute-done.29.refs_2_ = bf16[1,384,512]{2,1,0:T(8,128)(2,1)S(1)} collective-permute-done((bf16[1,384,512]{2,1,0:T(8,128)(2,1)S(1)}, bf16[1,384,512]{2,1,0:T(8,128)(2,1)S(1)}, u32[]{:S(2)}, u32[]{:S(2)}) %collective-permute-start.29) | collective-permute-done | bytes 393248 | tf_op jit(solution)/shard_map/ppermute | solution.py:25
  261.1 5.8 %shard_map.128 = (bf16[2,384,256]{2,1,0:T(8,128)(2,1)}, f32[2,384,256]{2,1,0:T(8,128)}) custom-call(s32[2]{0:T(128)} %pad_add_fusion.own_ref, bf16[4,384,640]{2,1,0:T(8,128)(2,1)} %add_convert_fusion.refs_0_, bf16[4,384,512]{2,1,0:T(8,128)(2,1)} %add_convert_fusion.2.refs_1_, bf16[4,384,512]{2,1,0:T(8,128)(2,1)} %add_convert_fusion.1.refs_2_, ...), custom_call_target="tpu_custom_call" | custom-call | flops 1000 | bytes 1000 | tf_op jit(solution)/shard_map/pallas_call | solution.py:174
  269.0 5.3 %shard_map.129 = (bf16[384,3072]{1,0:T(8,128)(2,1)}, bf16[384,3072]{1,0:T(8,128)(2,1)}, bf16[384,3072]{1,0:T(8,128)(2,1)}) custom-call(f32[2,384,512]{2,1,0:T(8,128)} %get-tuple-element.140.refs_0_, bf16[2,384,512]{2,1,0:T(8,128)(2,1)} %copy-done.11, bf16[1,384,512]{2,1,0:T(8,128)(2,1)} %copy-done.31, ...), custom_call_target="tpu_custom_call", output_to_operand_aliasing={{0}: (8, {}), {1}: (9, {}), {2}: (10, {})} | custom-call | flops 1000 | bytes 1000 | tf_op jit(solution)/shard_map/pallas_call | solution.py:240
  274.3 4.7 %collective-permute-done.31.refs_2_ = bf16[1,384,512]{2,1,0:T(8,128)(2,1)S(1)} collective-permute-done((bf16[1,384,512]{2,1,0:T(8,128)(2,1)S(1)}, bf16[1,384,512]{2,1,0:T(8,128)(2,1)S(1)}, u32[]{:S(2)}, u32[]{:S(2)}) %collective-permute-start.31) | collective-permute-done | bytes 393248 | tf_op jit(solution)/shard_map/ppermute | solution.py:25
  281.7 5.3 %shard_map.130 = (bf16[384,3072]{1,0:T(8,128)(2,1)}, bf16[384,3072]{1,0:T(8,128)(2,1)}, bf16[384,3072]{1,0:T(8,128)(2,1)}) custom-call(f32[2,384,512]{2,1,0:T(8,128)} %get-tuple-element.145.refs_0_, bf16[2,384,512]{2,1,0:T(8,128)(2,1)} %copy-done.12, bf16[1,384,512]{2,1,0:T(8,128)(2,1)} %copy-done.33, ...), custom_call_target="tpu_custom_call", output_to_operand_aliasing={{0}: (8, {}), {1}: (9, {}), {2}: (10, {})} | custom-call | flops 1000 | bytes 1000 | tf_op jit(solution)/shard_map/pallas_call | solution.py:240
  287.0 5.5 %collective-permute-done.33.refs_1_ = bf16[2,384,256]{2,1,0:T(8,128)(2,1)S(1)} collective-permute-done((bf16[2,384,256]{2,1,0:T(8,128)(2,1)}, bf16[2,384,256]{2,1,0:T(8,128)(2,1)S(1)}, u32[]{:S(2)}, u32[]{:S(2)}) %collective-permute-start.33) | collective-permute-done | bytes 393248 | tf_op jit(solution)/shard_map/ppermute | solution.py:25
  (191 shorter events, 127.8 us)
Async XLA Ops:
  7.2 123.3 %all-gather.8.cloned.1.call-start = ((), (), s32[]{:S(2)}) async-start(), calls=%async_computation.2 | async-start | bytes 4259840 | tf_op jit(solution)/shard_map/all_gather | solution.py:325
  10.6 152.8 %all-gather.6.cloned.1.call-start = ((), (), s32[]{:S(2)}) async-start(), calls=%async_computation.1 | async-start | bytes 4259840 | tf_op jit(solution)/shard_map/all_gather | solution.py:325
  34.7 18.0 %collective-permute-start.6 = (bf16[2,192,640]{2,1,0:T(8,128)(2,1)}, bf16[2,192,640]{2,1,0:T(8,128)(2,1)S(1)}, u32[]{:S(2)}, u32[]{:S(2)}) collective-permute-start(bf16[2,192,640]{2,1,0:T(8,128)(2,1)} %get-tuple-element.83), channel_id=1, source_target_pairs={{0,2},{1,3},{2,0},{3,1},{4,6},{5,7},{6,4},{7,5},{8,10},{9,11},{10,... | collective-permute-start | bytes 1474568 | tf_op jit(solution)/shard_map/ppermute | solution.py:25
  36.9 21.2 %collective-permute-start.7 = (bf16[2,192,640]{2,1,0:T(8,128)(2,1)}, bf16[2,192,640]{2,1,0:T(8,128)(2,1)S(1)}, u32[]{:S(2)}, u32[]{:S(2)}) collective-permute-start(bf16[2,192,640]{2,1,0:T(8,128)(2,1)} %get-tuple-element.84), channel_id=1, source_target_pairs={{0,4},{1,5},{2,6},{3,7},{4,0},{5,1},{6,2},{7,3},{8,12},{9,13},{10,... | collective-permute-start | bytes 1474568 | tf_op jit(solution)/shard_map/ppermute | solution.py:25
  38.4 30.8 %collective-permute-start.8 = (bf16[2,192,640]{2,1,0:T(8,128)(2,1)}, bf16[2,192,640]{2,1,0:T(8,128)(2,1)S(1)}, u32[]{:S(2)}, u32[]{:S(2)}) collective-permute-start(bf16[2,192,640]{2,1,0:T(8,128)(2,1)} %get-tuple-element.85), channel_id=1, source_target_pairs={{0,6},{1,7},{2,4},{3,5},{4,2},{5,3},{6,0},{7,1},{8,14},{9,15},{10,... | collective-permute-start | bytes 1474568 | tf_op jit(solution)/shard_map/ppermute | solution.py:25
  39.8 34.8 %collective-permute-start.16 = (bf16[384,512]{1,0:T(8,128)(2,1)}, bf16[384,512]{1,0:T(8,128)(2,1)S(1)}, u32[]{:S(2)}, u32[]{:S(2)}) collective-permute-start(bf16[384,512]{1,0:T(8,128)(2,1)} %get-tuple-element.94), channel_id=1, source_target_pairs={{0,0},{1,16},{2,2},{3,18},{4,4},{5,20},{6,6},{7,22},{8,8},{9,24},{... | collective-permute-start | bytes 1179656 | tf_op jit(solution)/shard_map/ppermute | solution.py:25
  48.9 25.7 %collective-permute-start.17 = (bf16[384,512]{1,0:T(8,128)(2,1)}, bf16[384,512]{1,0:T(8,128)(2,1)S(1)}, u32[]{:S(2)}, u32[]{:S(2)}) collective-permute-start(bf16[384,512]{1,0:T(8,128)(2,1)} %get-tuple-element.96), channel_id=1, source_target_pairs={{0,8},{1,24},{2,10},{3,26},{4,12},{5,28},{6,14},{7,30},{8,0},{9,16... | collective-permute-start | bytes 1179656 | tf_op jit(solution)/shard_map/ppermute | solution.py:25
  52.7 29.1 %collective-permute-start.12 = (bf16[2,192,512]{2,1,0:T(8,128)(2,1)}, bf16[2,192,512]{2,1,0:T(8,128)(2,1)S(1)}, u32[]{:S(2)}, u32[]{:S(2)}) collective-permute-start(bf16[2,192,512]{2,1,0:T(8,128)(2,1)} %get-tuple-element.91), channel_id=1, source_target_pairs={{0,2},{1,3},{2,0},{3,1},{4,6},{5,7},{6,4},{7,5},{8,10},{9,11},{10,... | collective-permute-start | bytes 1179656 | tf_op jit(solution)/shard_map/ppermute | solution.py:25
  58.1 30.1 %collective-permute-start.13 = (bf16[2,192,512]{2,1,0:T(8,128)(2,1)}, bf16[2,192,512]{2,1,0:T(8,128)(2,1)S(1)}, u32[]{:S(2)}, u32[]{:S(2)}) collective-permute-start(bf16[2,192,512]{2,1,0:T(8,128)(2,1)} %get-tuple-element.92), channel_id=1, source_target_pairs={{0,4},{1,5},{2,6},{3,7},{4,0},{5,1},{6,2},{7,3},{8,12},{9,13},{10,... | collective-permute-start | bytes 1179656 | tf_op jit(solution)/shard_map/ppermute | solution.py:25
  69.2 19.4 %collective-permute-start.14 = (bf16[2,192,512]{2,1,0:T(8,128)(2,1)}, bf16[2,192,512]{2,1,0:T(8,128)(2,1)S(1)}, u32[]{:S(2)}, u32[]{:S(2)}) collective-permute-start(bf16[2,192,512]{2,1,0:T(8,128)(2,1)} %get-tuple-element.93), channel_id=1, source_target_pairs={{0,6},{1,7},{2,4},{3,5},{4,2},{5,3},{6,0},{7,1},{8,14},{9,15},{10,... | collective-permute-start | bytes 1179656 | tf_op jit(solution)/shard_map/ppermute | solution.py:25
  81.8 23.4 %collective-permute-start.20 = (bf16[2,192,512]{2,1,0:T(8,128)(2,1)}, bf16[2,192,512]{2,1,0:T(8,128)(2,1)S(1)}, u32[]{:S(2)}, u32[]{:S(2)}) collective-permute-start(bf16[2,192,512]{2,1,0:T(8,128)(2,1)} %get-tuple-element.101), channel_id=1, source_target_pairs={{0,6},{1,7},{2,4},{3,5},{4,2},{5,3},{6,0},{7,1},{8,14},{9,15},{10,... | collective-permute-start | bytes 1179656 | tf_op jit(solution)/shard_map/ppermute | solution.py:25
  110.4 101.8 %all-gather.4.cloned.1.call-start = ((), (), s32[]{:S(2)}) async-start(), calls=%async_computation | async-start | bytes 4259840 | tf_op jit(solution)/shard_map/all_gather | solution.py:325
  137.8 20.6 %collective-permute-start.22 = (bf16[2,384,512]{2,1,0:T(8,128)(2,1)}, bf16[2,384,512]{2,1,0:T(8,128)(2,1)S(1)}, u32[]{:S(2)}, u32[]{:S(2)}) collective-permute-start(bf16[2,384,512]{2,1,0:T(8,128)(2,1)} %get-tuple-element.106), channel_id=1, source_target_pairs={{0,8},{1,9},{2,10},{3,11},{4,12},{5,13},{6,14},{7,15},{8,0},{9,1},... | collective-permute-start | bytes 2359304 | tf_op jit(solution)/shard_map/ppermute | solution.py:25
  146.6 37.1 %collective-permute-start.24 = (bf16[2,384,512]{2,1,0:T(8,128)(2,1)}, bf16[2,384,512]{2,1,0:T(8,128)(2,1)S(1)}, u32[]{:S(2)}, u32[]{:S(2)}) collective-permute-start(bf16[2,384,512]{2,1,0:T(8,128)(2,1)} %get-tuple-element.108), channel_id=1, source_target_pairs={{0,8},{1,9},{2,10},{3,11},{4,12},{5,13},{6,14},{7,15},{8,0},{9,1},... | collective-permute-start | bytes 2359304 | tf_op jit(solution)/shard_map/ppermute | solution.py:25
  159.3 23.0 %collective-permute-start.23 = (bf16[1,384,512]{2,1,0:T(8,128)(2,1)S(1)}, bf16[1,384,512]{2,1,0:T(8,128)(2,1)S(1)}, u32[]{:S(2)}, u32[]{:S(2)}) collective-permute-start(bf16[1,384,512]{2,1,0:T(8,128)(2,1)S(1)} %add_convert_fusion.7), channel_id=1, source_target_pairs={{0,16},{1,17},{2,18},{3,19},{4,20},{5,21},{6,22},{7,23},{8,24},{9,... | collective-permute-start | bytes 1179656 | tf_op jit(solution)/shard_map/ppermute | solution.py:25
  170.9 38.2 %collective-permute-start.26 = (bf16[2,384,512]{2,1,0:T(8,128)(2,1)}, bf16[2,384,512]{2,1,0:T(8,128)(2,1)}, u32[]{:S(2)}, u32[]{:S(2)}) collective-permute-start(bf16[2,384,512]{2,1,0:T(8,128)(2,1)} %get-tuple-element.113), channel_id=1, source_target_pairs={{0,8},{1,9},{2,10},{3,11},{4,12},{5,13},{6,14},{7,15},{8,0},{9,1},... | collective-permute-start | bytes 2359304 | tf_op jit(solution)/shard_map/ppermute | solution.py:25
  183.8 23.7 %collective-permute-start.25 = (bf16[1,384,512]{2,1,0:T(8,128)(2,1)S(1)}, bf16[1,384,512]{2,1,0:T(8,128)(2,1)S(1)}, u32[]{:S(2)}, u32[]{:S(2)}) collective-permute-start(bf16[1,384,512]{2,1,0:T(8,128)(2,1)S(1)} %add_convert_fusion.6), channel_id=1, source_target_pairs={{0,16},{1,17},{2,18},{3,19},{4,20},{5,21},{6,22},{7,23},{8,24},{9,... | collective-permute-start | bytes 1179656 | tf_op jit(solution)/shard_map/ppermute | solution.py:25
  193.4 40.9 %collective-permute-start.28 = (bf16[2,384,512]{2,1,0:T(8,128)(2,1)}, bf16[2,384,512]{2,1,0:T(8,128)(2,1)S(1)}, u32[]{:S(2)}, u32[]{:S(2)}) collective-permute-start(bf16[2,384,512]{2,1,0:T(8,128)(2,1)} %get-tuple-element.116), channel_id=1, source_target_pairs={{0,8},{1,9},{2,10},{3,11},{4,12},{5,13},{6,14},{7,15},{8,0},{9,1},... | collective-permute-start | bytes 2359304 | tf_op jit(solution)/shard_map/ppermute | solution.py:25
  210.2 22.6 %collective-permute-start.27 = (bf16[1,384,512]{2,1,0:T(8,128)(2,1)S(1)}, bf16[1,384,512]{2,1,0:T(8,128)(2,1)S(1)}, u32[]{:S(2)}, u32[]{:S(2)}) collective-permute-start(bf16[1,384,512]{2,1,0:T(8,128)(2,1)S(1)} %add_convert_fusion.5), channel_id=1, source_target_pairs={{0,16},{1,17},{2,18},{3,19},{4,20},{5,21},{6,22},{7,23},{8,24},{9,... | collective-permute-start | bytes 1179656 | tf_op jit(solution)/shard_map/ppermute | solution.py:25
  219.7 39.3 %collective-permute-start.30 = (bf16[2,384,512]{2,1,0:T(8,128)(2,1)}, bf16[2,384,512]{2,1,0:T(8,128)(2,1)S(1)}, u32[]{:S(2)}, u32[]{:S(2)}) collective-permute-start(bf16[2,384,512]{2,1,0:T(8,128)(2,1)} %get-tuple-element.123), channel_id=1, source_target_pairs={{0,8},{1,9},{2,10},{3,11},{4,12},{5,13},{6,14},{7,15},{8,0},{9,1},... | collective-permute-start | bytes 2359304 | tf_op jit(solution)/shard_map/ppermute | solution.py:25
  234.4 23.2 %collective-permute-start.29 = (bf16[1,384,512]{2,1,0:T(8,128)(2,1)S(1)}, bf16[1,384,512]{2,1,0:T(8,128)(2,1)S(1)}, u32[]{:S(2)}, u32[]{:S(2)}) collective-permute-start(bf16[1,384,512]{2,1,0:T(8,128)(2,1)S(1)} %add_convert_fusion.4), channel_id=1, source_target_pairs={{0,16},{1,17},{2,18},{3,19},{4,20},{5,21},{6,22},{7,23},{8,24},{9,... | collective-permute-start | bytes 1179656 | tf_op jit(solution)/shard_map/ppermute | solution.py:25
  259.1 19.9 %collective-permute-start.31 = (bf16[1,384,512]{2,1,0:T(8,128)(2,1)S(1)}, bf16[1,384,512]{2,1,0:T(8,128)(2,1)S(1)}, u32[]{:S(2)}, u32[]{:S(2)}) collective-permute-start(bf16[1,384,512]{2,1,0:T(8,128)(2,1)S(1)} %add_convert_fusion.3), channel_id=1, source_target_pairs={{0,16},{1,17},{2,18},{3,19},{4,20},{5,21},{6,22},{7,23},{8,24},{9,... | collective-permute-start | bytes 1179656 | tf_op jit(solution)/shard_map/ppermute | solution.py:25
  261.1 20.4 %collective-permute-start.32 = (bf16[2,384,256]{2,1,0:T(8,128)(2,1)S(1)}, bf16[2,384,256]{2,1,0:T(8,128)(2,1)S(1)}, u32[]{:S(2)}, u32[]{:S(2)}) collective-permute-start(bf16[2,384,256]{2,1,0:T(8,128)(2,1)S(1)} %copy-done.42), channel_id=1, source_target_pairs={{0,8},{1,9},{2,10},{3,11},{4,12},{5,13},{6,14},{7,15},{8,0},{9,1},... | collective-permute-start | bytes 1179656 | tf_op jit(solution)/shard_map/ppermute | solution.py:25
  266.9 25.5 %collective-permute-start.33 = (bf16[2,384,256]{2,1,0:T(8,128)(2,1)}, bf16[2,384,256]{2,1,0:T(8,128)(2,1)S(1)}, u32[]{:S(2)}, u32[]{:S(2)}) collective-permute-start(bf16[2,384,256]{2,1,0:T(8,128)(2,1)} %get-tuple-element.139), channel_id=1, source_target_pairs={{0,8},{1,9},{2,10},{3,11},{4,12},{5,13},{6,14},{7,15},{8,0},{9,1},... | collective-permute-start | bytes 1179656 | tf_op jit(solution)/shard_map/ppermute | solution.py:25
  (58 other events, 490.7 us)
Sparse Core Ops, SparseCore 0:
  10.7 68.0 all-gather.7
  110.5 52.8 all-gather.5
  165.3 46.2 all-gather.3
